TPU v7x, 512 devices: a whole 4x4x16 slice. The times are simulated.
512 devices in a mesh: replica: 8 (over z_lo), fsdp: 64 (over z_hi, y, x, core).
Axes of the slice: x: 4, y: 4, z: 16 (z_hi: 2, z_lo: 8; z = z_hi * 8 + z_lo), core: 2. Of those that a mesh axis runs over, the one named last changes fastest.
Arguments:
- activations: bfloat16 [65536, 6144], P(('replica', 'fsdp')), may hold values from -400 to 400
- targets: bfloat16 [65536, 512], P(('replica', 'fsdp')), may hold values from -6 to 6
- weights: float32 [8, 6144, 512], P('replica', 'fsdp'), may hold values from -0.078125 to 0.078125
- first_moment: float32 [8, 6144, 512], P('replica', 'fsdp'), may hold values from -4 to 4
- second_moment: float32 [8, 6144, 512], P('replica', 'fsdp'), may hold values from 0.05 to 1
- local_frags: float32 [8, 2, 6144, 128], P('replica', None, 'fsdp'), may hold values from -6 to 6
- global_frags: float32 [2, 6144, 128], P(None, 'fsdp'), may hold values from -6 to 6
- momentum_frags: float32 [2, 6144, 128], P(None, 'fsdp'), may hold values from -6 to 6
- fragment_index: int32 [1], replicated, may hold values from 0 to 1
Outputs:
- new_weights: float32 [8, 6144, 512], P('replica', 'fsdp')
- new_first: float32 [8, 6144, 512], P('replica', 'fsdp')
- new_second: float32 [8, 6144, 512], P('replica', 'fsdp')
- new_global: float32 [6144, 128], P('fsdp')
- new_momentum: float32 [6144, 128], P('fsdp')
All inputs are finite; a program needn't handle non-finite values.
Results may differ from a plain program's by a relative error of at most 0.0045.
Values may be sent and summed in bfloat16 or wider, within the bound.
No kernel may reach another device: no remote copies, remote signals or barrier semaphores. Data moves between devices by JAX's collectives and lax.ppermute only.
A program may use at most 64 MiB of HBM per device.

v0:
```python
import math

import jax
import jax.numpy as jnp
from jax import lax
from jax.sharding import PartitionSpec as P


def on_device(
    activations,
    targets,
    weights,
    first_moment,
    second_moment,
    local_frags,
    global_frags,
    momentum_frags,
    fragment_index,
):
    wide = activations.astype(jnp.float32)
    normed = (wide * lax.rsqrt(jnp.mean(wide * wide, axis=1, keepdims=True) + 1e-05)).astype(
        jnp.bfloat16
    )
    master = weights[0]
    low_weights = master.astype(jnp.bfloat16)
    values = jnp.dot(
        normed,
        lax.all_gather(low_weights, "fsdp", axis=0, tiled=True),
        preferred_element_type=jnp.float32,
    )
    fsdp_count = lax.axis_size("fsdp")
    factor = 1.0 / math.sqrt(normed.shape[0] * fsdp_count)
    cotangent = ((values - targets.astype(jnp.float32)) * factor).astype(jnp.bfloat16)
    every_cotangent = lax.all_gather(cotangent, "fsdp", axis=0, tiled=True)
    feature_block = lax.all_to_all(normed, "fsdp", split_axis=1, concat_axis=0, tiled=True)
    gradient = lax.dot_general(
        feature_block, every_cotangent, (((0,), (0,)), ((), ())), preferred_element_type=jnp.float32
    )
    new_first = 0.9 * first_moment[0] + 0.1 * gradient
    new_second = 0.95 * second_moment[0] + 0.05 * gradient * gradient
    new_master = master - 0.01 * (new_first / (jnp.sqrt(new_second) + 1e-08) + 0.1 * master)
    chosen = fragment_index[0]
    local_part = lax.dynamic_index_in_dim(local_frags[0], chosen, 0, False)
    global_part = lax.dynamic_index_in_dim(global_frags, chosen, 0, False)
    moment_part = lax.dynamic_index_in_dim(momentum_frags, chosen, 0, False)
    delta = global_part - local_part
    replicas = lax.axis_size("replica")
    mean_delta = lax.psum(delta, "replica") / replicas
    new_momentum = 0.9 * moment_part + mean_delta
    new_global = global_part - 0.7 * (mean_delta + 0.9 * new_momentum)
    return (new_master[None], new_first[None], new_second[None], new_global, new_momentum)


def solution(mesh):
    return jax.shard_map(
        on_device,
        mesh=mesh,
        in_specs=(
            P(("replica", "fsdp"), None),
            P(("replica", "fsdp"), None),
            P("replica", "fsdp", None),
            P("replica", "fsdp", None),
            P("replica", "fsdp", None),
            P("replica", None, "fsdp", None),
            P(None, "fsdp", None),
            P(None, "fsdp", None),
            P(),
        ),
        out_specs=(
            P("replica", "fsdp", None),
            P("replica", "fsdp", None),
            P("replica", "fsdp", None),
            P("fsdp", None),
            P("fsdp", None),
        ),
        check_vma=False,
    )
```

profile of v0, /device:TPU:97, one launch (start us, length us, event | category | flops | bytes accessed | tf_op | source)
XLA Modules:
  0.0 398.3 jit_solution(11961329071704310374)
XLA Ops:
  7.2 0.0 all-gather.3.cloned.1.call-start
  7.2 1.6 bitcast_convert_fusion
  8.8 0.0 all-gather.3.cloned.1.call-update
  8.8 0.0 all-gather.5.cloned.1.call-start
  8.9 1.9 copy.14
  10.8 0.8 fusion
  11.6 1.5 fusion.1
  13.1 154.3 %all-gather.3.cloned.1.call-done = bf16[6144,512]{1,0:T(8,128)(2,1)} async-done(((bf16[96,512]{1,0:T(8,128)(2,1)}), bf16[6144,512]{1,0:T(8,128)(2,1)}) %all-gather.3.cloned.1.call-update) | async-done | bytes 6291472 | tf_op jit(solution)/shard_map/all_gather | solution.py:28
  167.4 0.0 copy-done.3
  167.4 5.0 %fusion.6 = bf16[128,512]{1,0:T(8,128)(2,1)} fusion(bf16[128,6144]{0,1:T(8,128)(2,1)} %fusion.1, bf16[6144,512]{1,0:T(8,128)(2,1)} %all-gather.3.cloned.1.call-done, bf16[128,512]{1,0:T(8,128)(2,1)S(1)} %copy-done.3), kind=kOutput, calls=%fused_computation.9 | convolution fusion | flops 805568512 | bytes 8126464 | tf_op jit(solution)/shard_map/dot_general | solution.py:26
  172.4 0.0 all-gather.5.cloned.1.call-update
  172.4 0.0 copy-start.4
  172.4 0.0 copy-start.5
  172.4 0.0 copy-start.6
  172.4 0.0 copy-start
  172.5 0.0 copy-start.1
  172.5 0.0 copy-start.2
  172.5 5.2 %all-to-all-start = ((bf16[128,64,96]{0,2,1:T(8,128)(2,1)}), bf16[128,64,96]{0,2,1:T(8,128)(2,1)S(1)}, u32[]{:S(2)}, u32[]{:S(2)}) async-start(bf16[128,64,96]{0,2,1:T(8,128)(2,1)} %bitcast.2), calls=%async_computation | async-start | bytes 3145728 | tf_op jit(solution)/shard_map/all_to_all | solution.py:35
  178.4 107.8 %psum.7 = f32[96,128]{1,0:T(8,128)S(1)} all-reduce(f32[96,128]{1,0:T(8,128)S(1)} %bitcast_subtract_fusion.1), channel_id=1, replica_groups=mesh['replica'=8,'fsdp'=64] {'replica'}, use_global_device_ids=true, to_apply=%region_1.2 | all-reduce | flops 12288 | bytes 98304 | tf_op jit(solution)/shard_map/psum | solution.py:48
  286.2 0.7 bitcast_subtract_fusion.2
  286.9 0.0 all-to-all-done
  286.9 98.8 %all-gather.5.cloned.1.call-done = bf16[8192,512]{1,0:T(8,128)(2,1)} async-done(((bf16[128,512]{1,0:T(8,128)(2,1)}), bf16[8192,512]{1,0:T(8,128)(2,1)}) %all-gather.5.cloned.1.call-update) | async-done | bytes 8388624 | tf_op jit(solution)/shard_map/all_gather | solution.py:34
  385.7 0.0 copy-done.1
  385.7 5.7 %fusion.12 = (f32[1,96,512]{2,1,0:T(8,128)}, f32[1,96,512]{2,1,0:T(8,128)}, f32[1,96,512]{2,1,0:T(8,128)}) fusion(f32[1,96,512]{2,1,0:T(8,128)S(1)} %copy-done.1, f32[1,96,512]{2,1,0:T(8,128)S(1)} %copy-done.2, f32[1,96,512]{2,1,0:T(8,128)S(1)} %copy-done, bf16[8192,512]{1,0:T(8,128)(2,1)} %all-gather.5.cloned.1.call-done, ...), kind=kOutput, calls=%fused_computation.20 | convolution fusion | flops 805945344 | bytes 11141120 | tf_op jit(solution)/shard_map/dot_general | solution.py:36
  (8 shorter events, 0.0 us)
Async XLA Ops:
  7.2 160.3 %all-gather.3.cloned.1.call-start = ((), (), s32[]{:S(2)}) async-start(), calls=%async_computation.1 | async-start | bytes 6389760 | tf_op jit(solution)/shard_map/all_gather | solution.py:28
  8.8 376.9 %all-gather.5.cloned.1.call-start = ((), (), s32[]{:S(2)}) async-start(), calls=%async_computation.2 | async-start | bytes 8519680 | tf_op jit(solution)/shard_map/all_gather | solution.py:34
  11.6 155.8 %copy-start.3 = (bf16[128,512]{1,0:T(8,128)(2,1)S(1)}, bf16[128,512]{1,0:T(8,128)(2,1)}, u32[]{:S(2)}) copy-start(bf16[128,512]{1,0:T(8,128)(2,1)} %param.10) | copy-start | bytes 393220
  172.4 6.0 %copy-start.4 = (f32[2,96,128]{2,1,0:T(8,128)S(1)}, f32[2,96,128]{2,1,0:T(8,128)}, u32[]{:S(2)}) copy-start(f32[2,96,128]{2,1,0:T(8,128)} %param.15) | copy-start | bytes 294916
  172.4 6.0 %copy-start.5 = (f32[1,2,96,128]{3,2,1,0:T(8,128)S(1)}, f32[1,2,96,128]{3,2,1,0:T(8,128)}, u32[]{:S(2)}) copy-start(f32[1,2,96,128]{3,2,1,0:T(8,128)} %param.14) | copy-start | bytes 294916
  172.4 113.8 %copy-start.6 = (f32[2,96,128]{2,1,0:T(8,128)S(1)}, f32[2,96,128]{2,1,0:T(8,128)}, u32[]{:S(2)}) copy-start(f32[2,96,128]{2,1,0:T(8,128)} %param.16) | copy-start | bytes 294916
  172.4 213.3 %copy-start = (f32[1,96,512]{2,1,0:T(8,128)S(1)}, f32[1,96,512]{2,1,0:T(8,128)}, u32[]{:S(2)}) copy-start(f32[1,96,512]{2,1,0:T(8,128)} %param.11) | copy-start | bytes 589828
  172.5 213.3 %copy-start.1 = (f32[1,96,512]{2,1,0:T(8,128)S(1)}, f32[1,96,512]{2,1,0:T(8,128)}, u32[]{:S(2)}) copy-start(f32[1,96,512]{2,1,0:T(8,128)} %param.13) | copy-start | bytes 589828
  172.5 213.3 %copy-start.2 = (f32[1,96,512]{2,1,0:T(8,128)S(1)}, f32[1,96,512]{2,1,0:T(8,128)}, u32[]{:S(2)}) copy-start(f32[1,96,512]{2,1,0:T(8,128)} %param.12) | copy-start | bytes 589828
  172.5 114.4 %all-to-all-start = ((bf16[128,64,96]{0,2,1:T(8,128)(2,1)}), bf16[128,64,96]{0,2,1:T(8,128)(2,1)S(1)}, u32[]{:S(2)}, u32[]{:S(2)}) async-start(bf16[128,64,96]{0,2,1:T(8,128)(2,1)} %bitcast.2), calls=%async_computation | async-start | bytes 3145728 | tf_op jit(solution)/shard_map/all_to_all | solution.py:35
Sparse Core Ops, SparseCore 0:
  13.2 154.2 all-gather.2
  172.6 213.1 all-gather.4
where the time goes:
time: 399 us; the launch traced here: 398 us
  waiting for transfers between devices  253 us (63%)
  blocking collectives  108 us (27%)
  between operations  14.8 us (4%)
  matrix products  10.7 us (3%)
  starting transfers between devices  5.3 us (1%)
  other arithmetic  4.58 us (1%)
    all_gather x1, waiting for transfers between devices, on_device(): lax.all_gather(low_weights, 'fsdp', axis=0, tiled=True)  154 us
    psum x1, blocking collectives, on_device(): mean_delta = lax.psum(delta, 'replica') / replicas  108 us
    all_gather x1, waiting for transfers between devices, on_device(): every_cotangent = lax.all_gather(cotangent, 'fsdp', axis=0, tiled=True)  98.8 us
  transfers between devices with their start and end apart: 3, of which 2 were waited for; matrix products, arithmetic and copies ran while one was open for 1% of the time, Pallas kernels for 0%

commit v1 on v0

v1 whole, which is shorter than its diff:
```python
import math

import jax
import jax.numpy as jnp
from jax import lax
from jax.sharding import Mesh
from jax.sharding import PartitionSpec as P

AXES = ("r", "z", "y", "x", "c")
FSDP = ("z", "y", "x", "c")


def swap(block, axes, distance):
    size = lax.axis_size(axes)
    return lax.ppermute(block, axes, [(i, i ^ distance) for i in range(size)])


def gather(block, axis):
    size = lax.axis_size(axis)
    return exchange(jnp.broadcast_to(block[None], (size, *block.shape)), axis)


def exchange(blocks, axes):
    return lax.all_to_all(blocks, axes, split_axis=0, concat_axis=0, tiled=True)


def on_device(
    activations,
    targets,
    weights,
    first_moment,
    second_moment,
    local_frags,
    global_frags,
    momentum_frags,
    fragment_index,
):
    f32, bf16 = jnp.float32, jnp.bfloat16
    nz, ny, nx, nc = (lax.axis_size(a) for a in FSDP)
    tokens, features = activations.shape
    rows, columns = weights.shape[1:]

    wide = activations.astype(f32)
    normed = (wide * lax.rsqrt(jnp.mean(wide * wide, axis=1, keepdims=True) + 1e-05)).astype(bf16)
    blocks = normed.T.reshape(nz, ny, nx, nc, rows, tokens).transpose(3, 2, 1, 0, 4, 5)
    blocks = blocks.reshape(nc * nx, ny * nz * rows, tokens)
    held = exchange(blocks, ("c", "x"))

    master = weights[0]
    low = gather(master.astype(bf16), "z")
    low = gather(low, "y").reshape(ny * nz * rows, columns)

    part = jnp.einsum("sft,fn->stn", held, low, preferred_element_type=f32)
    part = part.reshape(nc, nx, tokens, columns).astype(bf16)
    part = jnp.sum(exchange(part, "c").astype(f32), axis=0)
    part = jnp.sum(exchange(part.astype(bf16), "x").astype(f32), axis=0)

    factor = 1.0 / math.sqrt(tokens * nz * ny * nx * nc)
    cotangent = ((part - targets.astype(f32)) * factor).astype(bf16)
    every = gather(gather(cotangent, "x"), "c").reshape(nc * nx, tokens, columns)

    grad = jnp.einsum("sft,stn->fn", held, every, preferred_element_type=f32)
    grad = grad.reshape(ny, nz, rows, columns).astype(bf16)
    grad = jnp.sum(exchange(grad, "y").astype(f32), axis=0)
    gradient = jnp.sum(exchange(grad.astype(bf16), "z").astype(f32), axis=0)

    new_first = 0.9 * first_moment[0] + 0.1 * gradient
    new_second = 0.95 * second_moment[0] + 0.05 * gradient * gradient
    new_master = master - 0.01 * (new_first / (jnp.sqrt(new_second) + 1e-08) + 0.1 * master)

    chosen = fragment_index[0]
    local_part = lax.dynamic_index_in_dim(local_frags[0], chosen, 0, False)
    global_part = lax.dynamic_index_in_dim(global_frags, chosen, 0, False)
    moment_part = lax.dynamic_index_in_dim(momentum_frags, chosen, 0, False)
    delta = global_part - local_part
    replicas = lax.axis_size("r")
    distance = 1
    while distance < replicas:
        delta = delta + swap(delta, "r", distance)
        distance *= 2
    mean_delta = delta / replicas
    new_momentum = 0.9 * moment_part + mean_delta
    new_global = global_part - 0.7 * (mean_delta + 0.9 * new_momentum)
    return (new_master[None], new_first[None], new_second[None], new_global, new_momentum)


def solution(mesh):
    grid = Mesh(mesh.devices.reshape(mesh.shape["replica"], 2, 4, 4, 2), AXES)
    return jax.shard_map(
        on_device,
        mesh=grid,
        in_specs=(
            P(AXES, None),
            P(AXES, None),
            P("r", FSDP, None),
            P("r", FSDP, None),
            P("r", FSDP, None),
            P("r", None, FSDP, None),
            P(None, FSDP, None),
            P(None, FSDP, None),
            P(),
        ),
        out_specs=(
            P("r", FSDP, None),
            P("r", FSDP, None),
            P("r", FSDP, None),
            P(FSDP, None),
            P(FSDP, None),
        ),
        check_vma=False,
    )
```

time: 399 us -> 165 us (0.41)
  the two profiles are of different devices: /device:TPU:97 before, /device:TPU:2 now
where the time goes in v1:
time: 165 us
  blocking collectives  57.1 us (35%)
  waiting for transfers between devices  52.4 us (32%)
  starting transfers between devices  41 us (25%)
  other arithmetic  5.07 us (3%)
  local copies, waits for them, and re-layouts  4.75 us (3%)
  matrix products  2.86 us (2%)
    all_to_all x5, blocking collectives, exchange(): return lax.all_to_all(blocks, axes, split_axis=0, concat_axis=0, tiled=True)  57.1 us
    all_to_all x4, waiting for transfers between devices, exchange(): return lax.all_to_all(blocks, axes, split_axis=0, concat_axis=0, tiled=True)  34.1 us
    all_to_all x4, starting transfers between devices, exchange(): return lax.all_to_all(blocks, axes, split_axis=0, concat_axis=0, tiled=True)  26.6 us
    ppermute x3, waiting for transfers between devices, swap(): return lax.ppermute(block, axes, [(i, i ^ distance) for i in range(size)])  18.3 us
    ppermute x3, starting transfers between devices, swap(): return lax.ppermute(block, axes, [(i, i ^ distance) for i in range(size)])  14.4 us
  transfers between devices with their start and end apart: 7, of which 6 were waited for; matrix products, arithmetic and copies ran while one was open for 2% of the time, Pallas kernels for 0%

profile of v1, /device:TPU:2, one launch (start us, length us, event | category | flops | bytes accessed | tf_op | source)
XLA Modules:
  0.0 164.6 jit_solution(6613124487511232986)
XLA Ops:
  0.6 0.9 convert_bitcast_fusion
  2.3 15.1 %all-to-all-start.1 = ((bf16[2,96,512]{2,1,0:T(8,128)(2,1)}), bf16[2,96,512]{2,1,0:T(8,128)(2,1)S(1)}, u32[]{:S(2)}, u32[]{:S(2)}) async-start(bf16[2,96,512]{2,1,0:T(8,128)(2,1)} %broadcast_in_dim.11), calls=%async_computation.1 | async-start | bytes 393216 | tf_op jit(solution)/shard_map/all_to_all | solution.py:24
  17.3 1.9 %copy.20 = bf16[128,6144]{0,1:T(8,128)(2,1)S(1)} copy(bf16[128,6144]{1,0:T(8,128)(2,1)} %param.9) | data formatting | bytes 3145728 | tf_op args[0]
  20.1 13.0 %all-to-all-done.1 = bf16[2,96,512]{2,1,0:T(8,128)(2,1)S(1)} async-done(((bf16[2,96,512]{2,1,0:T(8,128)(2,1)}), bf16[2,96,512]{2,1,0:T(8,128)(2,1)S(1)}, u32[]{:S(2)}, u32[]{:S(2)}) %all-to-all-start.1) | async-done | bytes 196640 | tf_op jit(solution)/shard_map/all_to_all | solution.py:24
  33.1 0.9 broadcast_in_dim.12
  34.1 4.5 %all-to-all-start.2 = ((bf16[4,2,96,512]{3,2,1,0:T(8,128)(2,1)}), bf16[4,2,96,512]{3,2,1,0:T(8,128)(2,1)S(1)}, u32[]{:S(2)}, u32[]{:S(2)}) async-start(bf16[4,2,96,512]{3,2,1,0:T(8,128)(2,1)} %broadcast_in_dim.12), calls=%async_computation.2 | async-start | bytes 1572864 | tf_op jit(solution)/shard_map/all_to_all | solution.py:24
  39.0 9.0 %all-to-all-done.2 = bf16[4,2,96,512]{3,2,1,0:T(8,128)(2,1)S(1)} async-done(((bf16[4,2,96,512]{3,2,1,0:T(8,128)(2,1)}), bf16[4,2,96,512]{3,2,1,0:T(8,128)(2,1)S(1)}, u32[]{:S(2)}, u32[]{:S(2)}) %all-to-all-start.2) | async-done | bytes 786464 | tf_op jit(solution)/shard_map/all_to_all | solution.py:24
  48.0 0.9 copy-done
  48.9 24.5 %all_to_all.45 = bf16[8,768,128]{2,1,0:T(8,128)(2,1)S(1)} all-to-all(bf16[8,768,128]{2,1,0:T(8,128)(2,1)S(1)} %bitcast.55), channel_id=1, replica_groups=mesh['r'=8,'z'=2,'y'=4,'x'=4,'c'=2] {'c','x'}, dimensions={0} | all-to-all | bytes 3145728 | tf_op jit(solution)/shard_map/all_to_all | solution.py:24
  73.4 1.0 convolution_convert_fusion
  74.5 4.6 %all_to_all.46 = bf16[2,4,128,512]{3,2,1,0:T(8,128)(2,1)S(1)} all-to-all(bf16[2,4,128,512]{3,2,1,0:T(8,128)(2,1)S(1)} %convolution_convert_fusion), channel_id=1, replica_groups=mesh['r'=8,'z'=2,'y'=4,'x'=4,'c'=2] {'c'}, dimensions={0} | all-to-all | bytes 2097152 | tf_op jit(solution)/shard_map/all_to_all | solution.py:24
  79.5 12.4 %all_to_all.47 = bf16[4,128,512]{2,1,0:T(8,128)(2,1)S(1)} all-to-all(bf16[4,128,512]{2,1,0:T(8,128)(2,1)S(1)} %reduce_sum.54), channel_id=1, replica_groups=mesh['r'=8,'z'=2,'y'=4,'x'=4,'c'=2] {'x'}, dimensions={0} | all-to-all | bytes 1048576 | tf_op jit(solution)/shard_map/all_to_all | solution.py:24
  92.0 11.0 %all_to_all.48 = bf16[4,128,512]{2,1,0:T(8,128)(2,1)S(1)} all-to-all(bf16[4,128,512]{2,1,0:T(8,128)(2,1)S(1)} %broadcast_in_dim.13), channel_id=1, replica_groups=mesh['r'=8,'z'=2,'y'=4,'x'=4,'c'=2] {'x'}, dimensions={0} | all-to-all | bytes 1048576 | tf_op jit(solution)/shard_map/all_to_all | solution.py:24
  103.1 4.6 %all_to_all.49 = bf16[2,4,128,512]{3,2,1,0:T(8,128)(2,1)S(1)} all-to-all(bf16[2,4,128,512]{3,2,1,0:T(8,128)(2,1)S(1)} %broadcast_in_dim.14), channel_id=1, replica_groups=mesh['r'=8,'z'=2,'y'=4,'x'=4,'c'=2] {'c'}, dimensions={0} | all-to-all | bytes 2097152 | tf_op jit(solution)/shard_map/all_to_all | solution.py:24
  107.7 1.9 %bitcast_convert_fusion = bf16[4,2,96,512]{3,2,1,0:T(8,128)(2,1)} fusion(bf16[4,2,96,8,128]{4,2,1,0,3:T(8,128)(2,1)S(1)} %bitcast.57, bf16[8,128,512,1,1]{2,1,4,3,0:T(8,128)(2,1)S(1)} %bitcast.60), kind=kOutput, calls=%fused_computation.4 | convolution fusion | flops 805699584 | bytes 3407872 | tf_op jit(solution)/shard_map/sft,stn->fn/dot_general | solution.py:62
  109.6 3.6 %all-to-all-start.7 = ((bf16[4,2,96,512]{3,2,1,0:T(8,128)(2,1)}), bf16[4,2,96,512]{3,2,1,0:T(8,128)(2,1)S(1)}, u32[]{:S(2)}, u32[]{:S(2)}) async-start(bf16[4,2,96,512]{3,2,1,0:T(8,128)(2,1)} %bitcast_convert_fusion), calls=%async_computation.7 | async-start | bytes 1572864 | tf_op jit(solution)/shard_map/all_to_all | solution.py:24
  114.0 12.1 %all-to-all-done.7 = bf16[4,2,96,512]{3,2,1,0:T(8,128)(2,1)S(1)} async-done(((bf16[4,2,96,512]{3,2,1,0:T(8,128)(2,1)}), bf16[4,2,96,512]{3,2,1,0:T(8,128)(2,1)S(1)}, u32[]{:S(2)}, u32[]{:S(2)}) %all-to-all-start.7) | async-done | bytes 786464 | tf_op jit(solution)/shard_map/all_to_all | solution.py:24
  126.9 3.4 %all-to-all-start.8 = ((bf16[2,96,512]{2,1,0:T(8,128)(2,1)}), bf16[2,96,512]{2,1,0:T(8,128)(2,1)S(1)}, u32[]{:S(2)}, u32[]{:S(2)}) async-start(bf16[2,96,512]{2,1,0:T(8,128)(2,1)} %reduce_sum.56), calls=%async_computation.8 | async-start | bytes 393216 | tf_op jit(solution)/shard_map/all_to_all | solution.py:24
  130.4 8.1 %collective-permute-start = (f32[96,128]{1,0:T(8,128)S(1)}, f32[96,128]{1,0:T(8,128)S(1)}, u32[]{:S(2)}, u32[]{:S(2)}) collective-permute-start(f32[96,128]{1,0:T(8,128)S(1)} %bitcast_subtract_fusion), channel_id=1, source_target_pairs={{0,64},{64,0},{128,192},{192,128},{256,320},{320,256},{384,448},{4... | collective-permute-start | bytes 147464 | tf_op jit(solution)/shard_map/ppermute | solution.py:15
  138.5 5.2 %collective-permute-done = f32[96,128]{1,0:T(8,128)S(1)} collective-permute-done((f32[96,128]{1,0:T(8,128)S(1)}, f32[96,128]{1,0:T(8,128)S(1)}, u32[]{:S(2)}, u32[]{:S(2)}) %collective-permute-start) | collective-permute-done | bytes 49184 | tf_op jit(solution)/shard_map/ppermute | solution.py:15
  143.7 1.9 %collective-permute-start.1 = (f32[96,128]{1,0:T(8,128)S(1)}, f32[96,128]{1,0:T(8,128)S(1)}, u32[]{:S(2)}, u32[]{:S(2)}) collective-permute-start(f32[96,128]{1,0:T(8,128)S(1)} %add.61), channel_id=1, source_target_pairs={{0,128},{64,192},{128,0},{192,64},{256,384},{320,448},{384,256},{4... | collective-permute-start | bytes 147464 | tf_op jit(solution)/shard_map/ppermute | solution.py:15
  145.6 7.0 %collective-permute-done.1 = f32[96,128]{1,0:T(8,128)S(1)} collective-permute-done((f32[96,128]{1,0:T(8,128)S(1)}, f32[96,128]{1,0:T(8,128)S(1)}, u32[]{:S(2)}, u32[]{:S(2)}) %collective-permute-start.1) | collective-permute-done | bytes 49184 | tf_op jit(solution)/shard_map/ppermute | solution.py:15
  152.6 4.3 %collective-permute-start.2 = (f32[96,128]{1,0:T(8,128)S(1)}, f32[96,128]{1,0:T(8,128)S(1)}, u32[]{:S(2)}, u32[]{:S(2)}) collective-permute-start(f32[96,128]{1,0:T(8,128)S(1)} %add.62), channel_id=1, source_target_pairs={{0,256},{64,320},{128,384},{192,448},{256,0},{320,64},{384,128},{4... | collective-permute-start | bytes 147464 | tf_op jit(solution)/shard_map/ppermute | solution.py:15
  156.9 6.1 %collective-permute-done.2 = f32[96,128]{1,0:T(8,128)S(1)} collective-permute-done((f32[96,128]{1,0:T(8,128)S(1)}, f32[96,128]{1,0:T(8,128)S(1)}, u32[]{:S(2)}, u32[]{:S(2)}) %collective-permute-start.2) | collective-permute-done | bytes 49184 | tf_op jit(solution)/shard_map/ppermute | solution.py:15
  (35 shorter events, 5.1 us)
Async XLA Ops:
  2.3 30.9 %all-to-all-start.1 = ((bf16[2,96,512]{2,1,0:T(8,128)(2,1)}), bf16[2,96,512]{2,1,0:T(8,128)(2,1)S(1)}, u32[]{:S(2)}, u32[]{:S(2)}) async-start(bf16[2,96,512]{2,1,0:T(8,128)(2,1)} %broadcast_in_dim.11), calls=%async_computation.1 | async-start | bytes 393216 | tf_op jit(solution)/shard_map/all_to_all | solution.py:24
  34.1 14.0 %all-to-all-start.2 = ((bf16[4,2,96,512]{3,2,1,0:T(8,128)(2,1)}), bf16[4,2,96,512]{3,2,1,0:T(8,128)(2,1)S(1)}, u32[]{:S(2)}, u32[]{:S(2)}) async-start(bf16[4,2,96,512]{3,2,1,0:T(8,128)(2,1)} %broadcast_in_dim.12), calls=%async_computation.2 | async-start | bytes 1572864 | tf_op jit(solution)/shard_map/all_to_all | solution.py:24
  48.0 0.9 copy-start
  48.9 24.5 %copy-start.1 = (bf16[4,2,96,512]{3,2,1,0:T(8,128)(2,1)S(1)}, bf16[4,2,96,512]{3,2,1,0:T(8,128)(2,1)}, u32[]{:S(2)}) copy-start(bf16[4,2,96,512]{3,2,1,0:T(8,128)(2,1)} %copy-done) | copy-start | bytes 2359300
  79.0 12.9 %copy-start.5 = (bf16[128,512]{1,0:T(8,128)(2,1)S(1)}, bf16[128,512]{1,0:T(8,128)(2,1)}, u32[]{:S(2)}) copy-start(bf16[128,512]{1,0:T(8,128)(2,1)} %param.10) | copy-start | bytes 393220
  109.6 20.7 %copy-start.6 = (f32[2,96,128]{2,1,0:T(8,128)S(1)}, f32[2,96,128]{2,1,0:T(8,128)}, u32[]{:S(2)}) copy-start(f32[2,96,128]{2,1,0:T(8,128)} %param.15) | copy-start | bytes 294916
  109.6 20.7 %copy-start.8 = (f32[1,2,96,128]{3,2,1,0:T(8,128)S(1)}, f32[1,2,96,128]{3,2,1,0:T(8,128)}, u32[]{:S(2)}) copy-start(f32[1,2,96,128]{3,2,1,0:T(8,128)} %param.14) | copy-start | bytes 294916
  109.6 53.5 %copy-start.7 = (f32[2,96,128]{2,1,0:T(8,128)S(1)}, f32[2,96,128]{2,1,0:T(8,128)}, u32[]{:S(2)}) copy-start(f32[2,96,128]{2,1,0:T(8,128)} %param.16) | copy-start | bytes 294916
  109.6 16.5 %all-to-all-start.7 = ((bf16[4,2,96,512]{3,2,1,0:T(8,128)(2,1)}), bf16[4,2,96,512]{3,2,1,0:T(8,128)(2,1)S(1)}, u32[]{:S(2)}, u32[]{:S(2)}) async-start(bf16[4,2,96,512]{3,2,1,0:T(8,128)(2,1)} %bitcast_convert_fusion), calls=%async_computation.7 | async-start | bytes 1572864 | tf_op jit(solution)/shard_map/all_to_all | solution.py:24
  113.2 50.5 %copy-start.2 = (f32[1,96,512]{2,1,0:T(8,128)S(1)}, f32[1,96,512]{2,1,0:T(8,128)}, u32[]{:S(2)}) copy-start(f32[1,96,512]{2,1,0:T(8,128)} %param.11) | copy-start | bytes 589828
  113.2 50.5 %copy-start.3 = (f32[1,96,512]{2,1,0:T(8,128)S(1)}, f32[1,96,512]{2,1,0:T(8,128)}, u32[]{:S(2)}) copy-start(f32[1,96,512]{2,1,0:T(8,128)} %param.13) | copy-start | bytes 589828
  113.2 50.5 %copy-start.4 = (f32[1,96,512]{2,1,0:T(8,128)S(1)}, f32[1,96,512]{2,1,0:T(8,128)}, u32[]{:S(2)}) copy-start(f32[1,96,512]{2,1,0:T(8,128)} %param.12) | copy-start | bytes 589828
  126.9 36.8 %all-to-all-start.8 = ((bf16[2,96,512]{2,1,0:T(8,128)(2,1)}), bf16[2,96,512]{2,1,0:T(8,128)(2,1)S(1)}, u32[]{:S(2)}, u32[]{:S(2)}) async-start(bf16[2,96,512]{2,1,0:T(8,128)(2,1)} %reduce_sum.56), calls=%async_computation.8 | async-start | bytes 393216 | tf_op jit(solution)/shard_map/all_to_all | solution.py:24
  130.4 13.3 %collective-permute-start = (f32[96,128]{1,0:T(8,128)S(1)}, f32[96,128]{1,0:T(8,128)S(1)}, u32[]{:S(2)}, u32[]{:S(2)}) collective-permute-start(f32[96,128]{1,0:T(8,128)S(1)} %bitcast_subtract_fusion), channel_id=1, source_target_pairs={{0,64},{64,0},{128,192},{192,128},{256,320},{320,256},{384,448},{4... | collective-permute-start | bytes 147464 | tf_op jit(solution)/shard_map/ppermute | solution.py:15
  143.7 8.9 %collective-permute-start.1 = (f32[96,128]{1,0:T(8,128)S(1)}, f32[96,128]{1,0:T(8,128)S(1)}, u32[]{:S(2)}, u32[]{:S(2)}) collective-permute-start(f32[96,128]{1,0:T(8,128)S(1)} %add.61), channel_id=1, source_target_pairs={{0,128},{64,192},{128,0},{192,64},{256,384},{320,448},{384,256},{4... | collective-permute-start | bytes 147464 | tf_op jit(solution)/shard_map/ppermute | solution.py:15
  152.6 10.4 %collective-permute-start.2 = (f32[96,128]{1,0:T(8,128)S(1)}, f32[96,128]{1,0:T(8,128)S(1)}, u32[]{:S(2)}, u32[]{:S(2)}) collective-permute-start(f32[96,128]{1,0:T(8,128)S(1)} %add.62), channel_id=1, source_target_pairs={{0,256},{64,320},{128,384},{192,448},{256,0},{320,64},{384,128},{4... | collective-permute-start | bytes 147464 | tf_op jit(solution)/shard_map/ppermute | solution.py:15

commit v2 on v1

v2 whole, which is shorter than its diff:
```python
import functools
import math

import jax
import jax.numpy as jnp
from jax import lax
from jax.experimental import pallas as pl
from jax.experimental.pallas import tpu as pltpu
from jax.sharding import Mesh
from jax.sharding import PartitionSpec as P

AXES = ("r", "z", "y", "x", "c")
FSDP = ("z", "y", "x", "c")
VMEM = pl.BlockSpec(memory_space=pltpu.VMEM)


def swap(block, axis, distance=1):
    size = lax.axis_size(axis)
    return lax.ppermute(block, axis, [(i, i ^ distance) for i in range(size)])


def exchange(blocks, axes):
    return lax.all_to_all(blocks, axes, split_axis=0, concat_axis=0, tiled=True)


def spread(block, axis):
    size = lax.axis_size(axis)
    return exchange(jnp.broadcast_to(block[None], (size, *block.shape)), axis)


def norm_kernel(sizes, act_ref, out_ref, chunk_ref, block_ref, in_sems, out_sems):
    nz, ny, nxc, rows = sizes
    tokens, features = act_ref.shape
    width = nxc * rows
    parts = range(nz * ny)
    arrive = [
        pltpu.make_async_copy(act_ref.at[:, pl.ds(i * width, width)], chunk_ref.at[i], in_sems.at[i])
        for i in parts
    ]
    leave = [
        pltpu.make_async_copy(block_ref.at[i], out_ref.at[:, i % ny, i // ny], out_sems.at[i])
        for i in parts
    ]
    for copy in arrive:
        copy.start()
    total = jnp.zeros((tokens, 1), jnp.float32)
    for i in parts:
        arrive[i].wait()
        part = chunk_ref[i].astype(jnp.float32)
        total = total + jnp.sum(part * part, axis=1, keepdims=True)
    scale = lax.rsqrt(total * (1.0 / features) + 1e-05)
    for i in parts:
        part = (chunk_ref[i].astype(jnp.float32) * scale).astype(jnp.bfloat16)
        block_ref[i] = part.T.reshape(nxc, rows, tokens)
        leave[i].start()
    for copy in leave:
        copy.wait()


def normed_blocks(activations, sizes):
    nz, ny, nxc, rows = sizes
    tokens = activations.shape[0]
    return pl.pallas_call(
        functools.partial(norm_kernel, sizes),
        out_shape=jax.ShapeDtypeStruct((nxc, ny, nz, rows, tokens), jnp.bfloat16),
        in_specs=[pl.BlockSpec(memory_space=pltpu.HBM)],
        out_specs=pl.BlockSpec(memory_space=pltpu.HBM),
        scratch_shapes=[
            pltpu.VMEM((nz * ny, tokens, nxc * rows), jnp.bfloat16),
            pltpu.VMEM((nz * ny, nxc, rows, tokens), jnp.bfloat16),
            pltpu.SemaphoreType.DMA((nz * ny,)),
            pltpu.SemaphoreType.DMA((nz * ny,)),
        ],
        compiler_params=pltpu.CompilerParams(vmem_limit_bytes=60 * 2**20),
        cost_estimate=pl.CostEstimate(
            flops=8 * activations.size, bytes_accessed=4 * activations.size, transcendentals=0
        ),
    )(activations)


def on_device(
    activations,
    targets,
    weights,
    first_moment,
    second_moment,
    local_frags,
    global_frags,
    momentum_frags,
    fragment_index,
):
    f32, bf16 = jnp.float32, jnp.bfloat16
    nz, ny, nx, nc = (lax.axis_size(a) for a in FSDP)
    z, c = lax.axis_index("z"), lax.axis_index("c")
    tokens, features = act_ref.shape
    width = nxc * rows
    parts = range(nz * ny)
    arrive = [
        pltpu.make_async_copy(act_ref.at[:, pl.ds(i * width, width)], chunk_ref.at[i], in_sems.at[i])
        for i in parts
    ]
    leave = [
        pltpu.make_async_copy(block_ref.at[i], out_ref.at[:, i % ny, i // ny], out_sems.at[i])
        for i in parts
    ]
    for copy in arrive:
        copy.start()
    total = jnp.zeros((tokens, 1), jnp.float32)
    for i in parts:
        arrive[i].wait()
        part = chunk_ref[i].astype(jnp.float32)
        total = total + jnp.sum(part * part, axis=1, keepdims=True)
    scale = lax.rsqrt(total * (1.0 / features) + 1e-05)
    for i in parts:
        part = (chunk_ref[i].astype(jnp.float32) * scale).astype(jnp.bfloat16)
        block_ref[i] = part.T.reshape(nxc, rows, tokens)
        leave[i].start()
    for copy in leave:
        copy.wait()


def normed_blocks(activations, sizes):
    nz, ny, nxc, rows = sizes
    tokens = activations.shape[0]
    return pl.pallas_call(
        functools.partial(norm_kernel, sizes),
        out_shape=jax.ShapeDtypeStruct((nxc, ny, nz, rows, tokens), jnp.bfloat16),
        in_specs=[pl.BlockSpec(memory_space=pltpu.HBM)],
        out_specs=pl.BlockSpec(memory_space=pltpu.HBM),
        scratch_shapes=[
            pltpu.VMEM((nz * ny, tokens, nxc * rows), jnp.bfloat16),
            pltpu.VMEM((nz * ny, nxc, rows, tokens), jnp.bfloat16),
            pltpu.SemaphoreType.DMA((nz * ny,)),
            pltpu.SemaphoreType.DMA((nz * ny,)),
        ],
        compiler_params=pltpu.CompilerParams(vmem_limit_bytes=60 * 2**20),
        cost_estimate=pl.CostEstimate(
            flops=8 * activations.size, bytes_accessed=4 * activations.size, transcendentals=0
        ),
    )(activations)


def on_device(
    activations,
    targets,
    weights,
    first_moment,
    second_moment,
    local_frags,
    global_frags,
    momentum_frags,
    fragment_index,
):
    f32, bf16 = jnp.float32, jnp.bfloat16
    nz, ny, nx, nc = (lax.axis_size(a) for a in FSDP)
    z, y, x, c = (lax.axis_index(a) for a in FSDP)
    tokens, features = activations.shape
    rows, columns = weights.shape[1:]
    group = ny * nz * rows

    chosen = fragment_index[0]
    local_part = lax.dynamic_index_in_dim(local_frags[0], chosen, 0, False)
    global_part = lax.dynamic_index_in_dim(global_frags, chosen, 0, False)
    moment_part = lax.dynamic_index_in_dim(momentum_frags, chosen, 0, False)
    delta = global_part - local_part

    master = weights[0]
    low = lax.all_gather(master.astype(bf16), "z")
    low = lax.all_gather(low, "y").reshape(group, columns)

    blocks = normed_blocks(activations, (nz, ny, nx * nc, rows))
    held = exchange(blocks.reshape(nx * nc, group, tokens), ("x", "c"))

    held = held.reshape(nx, nc, group, tokens)
    mine = lax.dynamic_index_in_dim(held, c, 1, False)
    theirs = lax.dynamic_index_in_dim(held, 1 - c, 1, False)

    send = jnp.einsum("sft,fn->stn", theirs, low, preferred_element_type=f32).astype(bf16)
    part = jnp.einsum("sft,fn->stn", mine, low, preferred_element_type=f32)
    part = lax.optimization_barrier(part) + swap(send, "c").astype(f32)
    part, delta = lax.optimization_barrier((part.astype(bf16), delta))
    arrived = swap(delta, "r", 1)
    part, arrived = lax.optimization_barrier((exchange(part, "x"), arrived))
    delta = delta + arrived
    part = part.astype(f32)
    factor = 1.0 / math.sqrt(tokens * nz * ny * nx * nc)
    cotangent = ((jnp.sum(part, axis=0) - targets.astype(f32)) * factor).astype(bf16)
    cotangent, delta = lax.optimization_barrier((cotangent, delta))
    arrived = swap(delta, "r", 2)
    near = spread(cotangent, "x")
    near, arrived = lax.optimization_barrier((near, arrived))
    delta = delta + arrived
    far = swap(near, "c")

    grad = jnp.einsum("sft,stn->fn", mine, near, preferred_element_type=f32)
    grad = grad + jnp.einsum("sft,stn->fn", theirs, far, preferred_element_type=f32)
    grad = grad.reshape(ny, nz, rows, columns).astype(bf16)
    delta, grad = lax.optimization_barrier((delta, grad))
    arrived = swap(delta, "r", 4)
    grad = exchange(grad, "y")
    grad, arrived = lax.optimization_barrier((grad, arrived))
    delta = delta + arrived
    grad = jnp.sum(grad.astype(f32), axis=0)
    sent = lax.dynamic_index_in_dim(grad, 1 - z, 0, False).astype(bf16)
    kept = lax.dynamic_index_in_dim(grad, z, 0, False)
    gradient = kept + swap(sent, "z").astype(f32)

    new_first = 0.9 * first_moment[0] + 0.1 * gradient
    new_second = 0.95 * second_moment[0] + 0.05 * gradient * gradient
    new_master = master - 0.01 * (new_first / (jnp.sqrt(new_second) + 1e-08) + 0.1 * master)

    mean_delta = delta / lax.axis_size("r")
    new_momentum = 0.9 * moment_part + mean_delta
    new_global = global_part - 0.7 * (mean_delta + 0.9 * new_momentum)
    return (new_master[None], new_first[None], new_second[None], new_global, new_momentum)


def solution(mesh):
    grid = Mesh(mesh.devices.reshape(mesh.shape["replica"], 2, 4, 4, 2), AXES)
    return jax.shard_map(
        on_device,
        mesh=grid,
        in_specs=(
            P(AXES, None),
            P(AXES, None),
            P("r", FSDP, None),
            P("r", FSDP, None),
            P("r", FSDP, None),
            P("r", None, FSDP, None),
            P(None, FSDP, None),
            P(None, FSDP, None),
            P(),
        ),
        out_specs=(
            P("r", FSDP, None),
            P("r", FSDP, None),
            P("r", FSDP, None),
            P(FSDP, None),
            P(FSDP, None),
        ),
        check_vma=False,
    )
```

time: 165 us -> 123 us (0.75)
  the two profiles are of different devices: /device:TPU:2 before, /device:TPU:33 now
where the time goes in v2:
time: 123 us; the launch traced here: 122 us
  starting transfers between devices  49.2 us (40%)
  blocking collectives  31.5 us (26%)
  waiting for transfers between devices  28.9 us (23%)
  other arithmetic  3.88 us (3%)
  Pallas kernels  3.35 us (3%)
  matrix products  3.25 us (3%)
  between operations  1.47 us (1%)
    ppermute x6, starting transfers between devices, swap(): return lax.ppermute(block, axis, [(i, i ^ distance) for i in range(size)])  31.8 us
    ppermute x6, waiting for transfers between devices, swap(): return lax.ppermute(block, axis, [(i, i ^ distance) for i in range(size)])  21.7 us
    all_gather x1, blocking collectives, on_device(): low = lax.all_gather(master.astype(bf16), 'z')  18.6 us
    all_to_all x4, starting transfers between devices, exchange(): return lax.all_to_all(blocks, axes, split_axis=0, concat_axis=0, tiled=True)  17.4 us
    all_gather x1, blocking collectives, on_device(): low = lax.all_gather(low, 'y').reshape(group, columns)  12.9 us
    all_to_all x4, waiting for transfers between devices, exchange(): return lax.all_to_all(blocks, axes, split_axis=0, concat_axis=0, tiled=True)  7.23 us
    pallas_call x1, Pallas kernels, normed_blocks(): pl.pallas_call(functools.partial(norm_kernel, sizes), out_shape=jax.Shape...  3.35 us
  transfers between devices with their start and end apart: 10, of which 9 were waited for; matrix products, arithmetic and copies ran while one was open for 2% of the time, Pallas kernels for 0%

profile of v2, /device:TPU:33, one launch (start us, length us, event | category | flops | bytes accessed | tf_op | source)
XLA Modules:
  0.0 122.5 jit_solution(17525276365176718171)
XLA Ops:
  0.6 3.3 %shard_map.128 = bf16[8,4,2,96,128]{4,3,2,1,0:T(8,128)(2,1)} custom-call(bf16[128,6144]{1,0:T(8,128)(2,1)} %act_ref.1), custom_call_target="tpu_custom_call" | custom-call | flops 6291456 | bytes 3145728 | tf_op jit(solution)/shard_map/pallas_call | solution.py:125
  4.0 5.1 %all-to-all-start = ((bf16[8,768,128]{2,1,0:T(8,128)(2,1)}), bf16[8,768,128]{2,1,0:T(8,128)(2,1)S(1)}, u32[]{:S(2)}, u32[]{:S(2)}) async-start(bf16[8,768,128]{2,1,0:T(8,128)(2,1)} %bitcast.93), calls=%async_computation | async-start | bytes 3145728 | tf_op jit(solution)/shard_map/all_to_all | solution.py:23
  9.1 18.6 %all_gather.10 = bf16[2,96,512]{2,1,0:T(8,128)(2,1)S(1)} all-gather(bf16[1,96,512]{2,1,0:T(8,128)(2,1)S(1)} %convert_element_type.40), channel_id=1, replica_groups=mesh['r'=8,'z'=2,'y'=4,'x'=4,'c'=2] {'z'}, dimensions={0}, use_global_device_ids=true | all-gather | bytes 294912 | tf_op jit(solution)/shard_map/all_gather | solution.py:168
  27.7 12.9 %all-gather = bf16[8,96,512]{2,1,0:T(8,128)(2,1)S(1)} all-gather(bf16[2,96,512]{2,1,0:T(8,128)(2,1)S(1)} %all_gather.10), channel_id=2, replica_groups=mesh['r'=8,'z'=2,'y'=4,'x'=4,'c'=2] {'y'}, dimensions={0}, use_global_device_ids=true | all-gather | bytes 983040 | tf_op jit(solution)/shard_map/all_gather | solution.py:169
  41.3 3.8 %collective-permute-start = (bf16[4,128,512]{2,1,0:T(8,128)(2,1)S(1)}, bf16[4,128,512]{2,1,0:T(8,128)(2,1)}, u32[]{:S(2)}, u32[]{:S(2)}) collective-permute-start(bf16[4,128,512]{2,1,0:T(8,128)(2,1)S(1)} %convolution_convert_fusion), channel_id=1, source_target_pairs={{0,1},{1,0},{2,3},{3,2},{4,5},{5,4},{6,7},{7,6},{8,9},{9,8},{10,11... | collective-permute-start | bytes 1572872 | tf_op jit(solution)/shard_map/ppermute | solution.py:19
  46.8 2.0 %add_convert_fusion = bf16[4,128,512]{2,1,0:T(8,128)(2,1)} fusion(f32[4,128,512]{2,1,0:T(8,128)S(1)} %fusion.5, bf16[4,128,512]{2,1,0:T(8,128)(2,1)} %collective-permute-done), kind=kLoop, calls=%fused_computation.5 | loop fusion | flops 786432 | bytes 2097152 | tf_op jit(solution)/shard_map/convert_element_type | solution.py:181
  48.8 4.3 %all-to-all-start.1 = ((bf16[4,128,512]{2,1,0:T(8,128)(2,1)}), bf16[4,128,512]{2,1,0:T(8,128)(2,1)S(1)}, u32[]{:S(2)}, u32[]{:S(2)}) async-start(bf16[4,128,512]{2,1,0:T(8,128)(2,1)} %add_convert_fusion), calls=%async_computation.1 | async-start | bytes 1048576 | tf_op jit(solution)/shard_map/all_to_all | solution.py:23
  53.1 1.9 %collective-permute-start.1 = (f32[96,128]{1,0:T(8,128)S(1)}, f32[96,128]{1,0:T(8,128)S(1)}, u32[]{:S(2)}, u32[]{:S(2)}) collective-permute-start(f32[96,128]{1,0:T(8,128)S(1)} %bitcast_subtract_fusion.1), channel_id=1, source_target_pairs={{0,64},{64,0},{128,192},{192,128},{256,320},{320,256},{384,448},{4... | collective-permute-start | bytes 147464 | tf_op jit(solution)/shard_map/ppermute | solution.py:19
  55.0 3.2 %collective-permute-done.1 = f32[96,128]{1,0:T(8,128)S(1)} collective-permute-done((f32[96,128]{1,0:T(8,128)S(1)}, f32[96,128]{1,0:T(8,128)S(1)}, u32[]{:S(2)}, u32[]{:S(2)}) %collective-permute-start.1) | collective-permute-done | bytes 49184 | tf_op jit(solution)/shard_map/ppermute | solution.py:19
  58.2 3.8 %all-to-all-done.1 = bf16[4,128,512]{2,1,0:T(8,128)(2,1)S(1)} async-done(((bf16[4,128,512]{2,1,0:T(8,128)(2,1)}), bf16[4,128,512]{2,1,0:T(8,128)(2,1)S(1)}, u32[]{:S(2)}, u32[]{:S(2)}) %all-to-all-start.1) | async-done | bytes 524320 | tf_op jit(solution)/shard_map/all_to_all | solution.py:23
  63.0 3.5 %all-to-all-start.2 = ((bf16[4,128,512]{2,1,0:T(8,128)(2,1)}), bf16[4,128,512]{2,1,0:T(8,128)(2,1)S(1)}, u32[]{:S(2)}, u32[]{:S(2)}) async-start(bf16[4,128,512]{2,1,0:T(8,128)(2,1)} %broadcast_in_dim.15), calls=%async_computation.2 | async-start | bytes 1048576 | tf_op jit(solution)/shard_map/all_to_all | solution.py:23
  66.4 1.9 %collective-permute-start.2 = (f32[96,128]{1,0:T(8,128)S(1)}, f32[96,128]{1,0:T(8,128)S(1)}, u32[]{:S(2)}, u32[]{:S(2)}) collective-permute-start(f32[96,128]{1,0:T(8,128)S(1)} %add.65), channel_id=1, source_target_pairs={{0,128},{64,192},{128,0},{192,64},{256,384},{320,448},{384,256},{4... | collective-permute-start | bytes 147464 | tf_op jit(solution)/shard_map/ppermute | solution.py:19
  68.4 3.8 %collective-permute-done.2 = f32[96,128]{1,0:T(8,128)S(1)} collective-permute-done((f32[96,128]{1,0:T(8,128)S(1)}, f32[96,128]{1,0:T(8,128)S(1)}, u32[]{:S(2)}, u32[]{:S(2)}) %collective-permute-start.2) | collective-permute-done | bytes 49184 | tf_op jit(solution)/shard_map/ppermute | solution.py:19
  72.2 1.9 %all-to-all-done.2 = bf16[4,128,512]{2,1,0:T(8,128)(2,1)S(1)} async-done(((bf16[4,128,512]{2,1,0:T(8,128)(2,1)}), bf16[4,128,512]{2,1,0:T(8,128)(2,1)S(1)}, u32[]{:S(2)}, u32[]{:S(2)}) %all-to-all-start.2) | async-done | bytes 524320 | tf_op jit(solution)/shard_map/all_to_all | solution.py:23
  74.1 4.6 %collective-permute-start.3 = (bf16[4,128,512]{2,1,0:T(8,128)(2,1)S(1)}, bf16[4,128,512]{2,1,0:T(8,128)(2,1)S(1)}, u32[]{:S(2)}, u32[]{:S(2)}) collective-permute-start(bf16[4,128,512]{2,1,0:T(8,128)(2,1)S(1)} %all-to-all-done.2), channel_id=1, source_target_pairs={{0,1},{1,0},{2,3},{3,2},{4,5},{5,4},{6,7},{7,6},{8,9},{9,8},{10,11... | collective-permute-start | bytes 1572872 | tf_op jit(solution)/shard_map/ppermute | solution.py:19
  79.3 0.9 collective-permute-done.3
  80.3 1.5 %fusion = bf16[768,512]{1,0:T(8,128)(2,1)} fusion(f32[768,512,1]{1,0,2:T(8,128)S(1)} %fusion.3, bf16[4,128,512]{2,1,0:T(8,128)(2,1)S(1)} %collective-permute-done.3, bf16[4,2,768,128]{3,2,1,0:T(8,128)(2,1)S(1)} %bitcast.90, s32[]{:T(128)S(6)} %select_n.21), kind=kOutput, calls=%fused_computation.1 | convolution fusion | flops 403439616 | bytes 3670020 | tf_op jit(solution)/shard_map/sft,stn->fn/dot_general | solution.py:196
  81.7 4.5 %all-to-all-start.3 = ((bf16[4,2,96,512]{3,2,1,0:T(8,128)(2,1)}), bf16[4,2,96,512]{3,2,1,0:T(8,128)(2,1)S(1)}, u32[]{:S(2)}, u32[]{:S(2)}) async-start(bf16[4,2,96,512]{3,2,1,0:T(8,128)(2,1)} %bitcast.14), calls=%async_computation.3 | async-start | bytes 1572864 | tf_op jit(solution)/shard_map/all_to_all | solution.py:23
  86.2 4.0 %collective-permute-start.4 = (f32[96,128]{1,0:T(8,128)S(1)}, f32[96,128]{1,0:T(8,128)S(1)}, u32[]{:S(2)}, u32[]{:S(2)}) collective-permute-start(f32[96,128]{1,0:T(8,128)S(1)} %add.66), channel_id=1, source_target_pairs={{0,256},{64,320},{128,384},{192,448},{256,0},{320,64},{384,128},{4... | collective-permute-start | bytes 147464 | tf_op jit(solution)/shard_map/ppermute | solution.py:19
  90.2 6.2 %collective-permute-done.4 = f32[96,128]{1,0:T(8,128)S(1)} collective-permute-done((f32[96,128]{1,0:T(8,128)S(1)}, f32[96,128]{1,0:T(8,128)S(1)}, u32[]{:S(2)}, u32[]{:S(2)}) %collective-permute-start.4) | collective-permute-done | bytes 49184 | tf_op jit(solution)/shard_map/ppermute | solution.py:19
  96.4 1.5 %all-to-all-done.3 = bf16[4,2,96,512]{3,2,1,0:T(8,128)(2,1)S(1)} async-done(((bf16[4,2,96,512]{3,2,1,0:T(8,128)(2,1)}), bf16[4,2,96,512]{3,2,1,0:T(8,128)(2,1)S(1)}, u32[]{:S(2)}, u32[]{:S(2)}) %all-to-all-start.3) | async-done | bytes 786464 | tf_op jit(solution)/shard_map/all_to_all | solution.py:23
  98.1 15.6 %collective-permute-start.5 = (bf16[96,512]{1,0:T(8,128)(2,1)S(1)}, bf16[96,512]{1,0:T(8,128)(2,1)S(1)}, u32[]{:S(2)}, u32[]{:S(2)}) collective-permute-start(bf16[96,512]{1,0:T(8,128)(2,1)S(1)} %fusion.15), channel_id=1, source_target_pairs={{0,32},{32,0},{1,33},{33,1},{2,34},{34,2},{3,35},{35,3},{4,36},{36... | collective-permute-start | bytes 294920 | tf_op jit(solution)/shard_map/ppermute | solution.py:19
  114.3 7.2 %collective-permute-done.5 = bf16[96,512]{1,0:T(8,128)(2,1)S(1)} collective-permute-done((bf16[96,512]{1,0:T(8,128)(2,1)S(1)}, bf16[96,512]{1,0:T(8,128)(2,1)S(1)}, u32[]{:S(2)}, u32[]{:S(2)}) %collective-permute-start.5) | collective-permute-done | bytes 98336 | tf_op jit(solution)/shard_map/ppermute | solution.py:19
  121.5 1.0 fusion.21
  (29 shorter events, 3.9 us)
Async XLA Ops:
  4.0 5.1 %copy-start = (f32[1,96,512]{2,1,0:T(8,128)S(1)}, f32[1,96,512]{2,1,0:T(8,128)}, u32[]{:S(2)}) copy-start(f32[1,96,512]{2,1,0:T(8,128)} %param.11) | copy-start | bytes 589828
  4.0 36.7 %all-to-all-start = ((bf16[8,768,128]{2,1,0:T(8,128)(2,1)}), bf16[8,768,128]{2,1,0:T(8,128)(2,1)S(1)}, u32[]{:S(2)}, u32[]{:S(2)}) async-start(bf16[8,768,128]{2,1,0:T(8,128)(2,1)} %bitcast.93), calls=%async_computation | async-start | bytes 3145728 | tf_op jit(solution)/shard_map/all_to_all | solution.py:23
  27.7 18.0 %copy-start.4 = (f32[2,96,128]{2,1,0:T(8,128)S(1)}, f32[2,96,128]{2,1,0:T(8,128)}, u32[]{:S(2)}) copy-start(f32[2,96,128]{2,1,0:T(8,128)} %param.15) | copy-start | bytes 294916
  27.7 18.0 %copy-start.6 = (f32[1,2,96,128]{3,2,1,0:T(8,128)S(1)}, f32[1,2,96,128]{3,2,1,0:T(8,128)}, u32[]{:S(2)}) copy-start(f32[1,2,96,128]{3,2,1,0:T(8,128)} %param.14) | copy-start | bytes 294916
  41.3 5.5 %collective-permute-start = (bf16[4,128,512]{2,1,0:T(8,128)(2,1)S(1)}, bf16[4,128,512]{2,1,0:T(8,128)(2,1)}, u32[]{:S(2)}, u32[]{:S(2)}) collective-permute-start(bf16[4,128,512]{2,1,0:T(8,128)(2,1)S(1)} %convolution_convert_fusion), channel_id=1, source_target_pairs={{0,1},{1,0},{2,3},{3,2},{4,5},{5,4},{6,7},{7,6},{8,9},{9,8},{10,11... | collective-permute-start | bytes 1572872 | tf_op jit(solution)/shard_map/ppermute | solution.py:19
  46.4 15.7 %copy-start.3 = (bf16[128,512]{1,0:T(8,128)(2,1)S(1)}, bf16[128,512]{1,0:T(8,128)(2,1)}, u32[]{:S(2)}) copy-start(bf16[128,512]{1,0:T(8,128)(2,1)} %param.10) | copy-start | bytes 393220
  48.8 13.2 %all-to-all-start.1 = ((bf16[4,128,512]{2,1,0:T(8,128)(2,1)}), bf16[4,128,512]{2,1,0:T(8,128)(2,1)S(1)}, u32[]{:S(2)}, u32[]{:S(2)}) async-start(bf16[4,128,512]{2,1,0:T(8,128)(2,1)} %add_convert_fusion), calls=%async_computation.1 | async-start | bytes 1048576 | tf_op jit(solution)/shard_map/all_to_all | solution.py:23
  53.1 5.1 %collective-permute-start.1 = (f32[96,128]{1,0:T(8,128)S(1)}, f32[96,128]{1,0:T(8,128)S(1)}, u32[]{:S(2)}, u32[]{:S(2)}) collective-permute-start(f32[96,128]{1,0:T(8,128)S(1)} %bitcast_subtract_fusion.1), channel_id=1, source_target_pairs={{0,64},{64,0},{128,192},{192,128},{256,320},{320,256},{384,448},{4... | collective-permute-start | bytes 147464 | tf_op jit(solution)/shard_map/ppermute | solution.py:19
  63.0 11.1 %all-to-all-start.2 = ((bf16[4,128,512]{2,1,0:T(8,128)(2,1)}), bf16[4,128,512]{2,1,0:T(8,128)(2,1)S(1)}, u32[]{:S(2)}, u32[]{:S(2)}) async-start(bf16[4,128,512]{2,1,0:T(8,128)(2,1)} %broadcast_in_dim.15), calls=%async_computation.2 | async-start | bytes 1048576 | tf_op jit(solution)/shard_map/all_to_all | solution.py:23
  66.4 5.7 %collective-permute-start.2 = (f32[96,128]{1,0:T(8,128)S(1)}, f32[96,128]{1,0:T(8,128)S(1)}, u32[]{:S(2)}, u32[]{:S(2)}) collective-permute-start(f32[96,128]{1,0:T(8,128)S(1)} %add.65), channel_id=1, source_target_pairs={{0,128},{64,192},{128,0},{192,64},{256,384},{320,448},{384,256},{4... | collective-permute-start | bytes 147464 | tf_op jit(solution)/shard_map/ppermute | solution.py:19
  74.1 6.2 %collective-permute-start.3 = (bf16[4,128,512]{2,1,0:T(8,128)(2,1)S(1)}, bf16[4,128,512]{2,1,0:T(8,128)(2,1)S(1)}, u32[]{:S(2)}, u32[]{:S(2)}) collective-permute-start(bf16[4,128,512]{2,1,0:T(8,128)(2,1)S(1)} %all-to-all-done.2), channel_id=1, source_target_pairs={{0,1},{1,0},{2,3},{3,2},{4,5},{5,4},{6,7},{7,6},{8,9},{9,8},{10,11... | collective-permute-start | bytes 1572872 | tf_op jit(solution)/shard_map/ppermute | solution.py:19
  81.7 31.9 %copy-start.5 = (f32[2,96,128]{2,1,0:T(8,128)S(1)}, f32[2,96,128]{2,1,0:T(8,128)}, u32[]{:S(2)}) copy-start(f32[2,96,128]{2,1,0:T(8,128)} %param.16) | copy-start | bytes 294916
  81.7 39.8 %copy-start.1 = (f32[1,96,512]{2,1,0:T(8,128)S(1)}, f32[1,96,512]{2,1,0:T(8,128)}, u32[]{:S(2)}) copy-start(f32[1,96,512]{2,1,0:T(8,128)} %param.13) | copy-start | bytes 589828
  81.7 39.8 %copy-start.2 = (f32[1,96,512]{2,1,0:T(8,128)S(1)}, f32[1,96,512]{2,1,0:T(8,128)}, u32[]{:S(2)}) copy-start(f32[1,96,512]{2,1,0:T(8,128)} %param.12) | copy-start | bytes 589828
  81.7 16.2 %all-to-all-start.3 = ((bf16[4,2,96,512]{3,2,1,0:T(8,128)(2,1)}), bf16[4,2,96,512]{3,2,1,0:T(8,128)(2,1)S(1)}, u32[]{:S(2)}, u32[]{:S(2)}) async-start(bf16[4,2,96,512]{3,2,1,0:T(8,128)(2,1)} %bitcast.14), calls=%async_computation.3 | async-start | bytes 1572864 | tf_op jit(solution)/shard_map/all_to_all | solution.py:23
  86.2 10.2 %collective-permute-start.4 = (f32[96,128]{1,0:T(8,128)S(1)}, f32[96,128]{1,0:T(8,128)S(1)}, u32[]{:S(2)}, u32[]{:S(2)}) collective-permute-start(f32[96,128]{1,0:T(8,128)S(1)} %add.66), channel_id=1, source_target_pairs={{0,256},{64,320},{128,384},{192,448},{256,0},{320,64},{384,128},{4... | collective-permute-start | bytes 147464 | tf_op jit(solution)/shard_map/ppermute | solution.py:19
  98.1 23.4 %collective-permute-start.5 = (bf16[96,512]{1,0:T(8,128)(2,1)S(1)}, bf16[96,512]{1,0:T(8,128)(2,1)S(1)}, u32[]{:S(2)}, u32[]{:S(2)}) collective-permute-start(bf16[96,512]{1,0:T(8,128)(2,1)S(1)} %fusion.15), channel_id=1, source_target_pairs={{0,32},{32,0},{1,33},{33,1},{2,34},{34,2},{3,35},{35,3},{4,36},{36... | collective-permute-start | bytes 294920 | tf_op jit(solution)/shard_map/ppermute | solution.py:19

commit v3 on v2

--- a/solution.py
+++ b/solution.py
@@ -31,7 +31,7 @@
 def norm_kernel(sizes, act_ref, out_ref, chunk_ref, block_ref, in_sems, out_sems):
     nz, ny, nxc, rows = sizes
     tokens, features = act_ref.shape
-    width = nxc * rows
+    width, lanes, step = nxc * rows, 128, 256
     parts = range(nz * ny)
     arrive = [
         pltpu.make_async_copy(act_ref.at[:, pl.ds(i * width, width)], chunk_ref.at[i], in_sems.at[i])
@@ -43,15 +43,30 @@
     ]
     for copy in arrive:
         copy.start()
-    total = jnp.zeros((tokens, 1), jnp.float32)
+    total = jnp.zeros((tokens, lanes), jnp.float32)
     for i in parts:
         arrive[i].wait()
-        part = chunk_ref[i].astype(jnp.float32)
-        total = total + jnp.sum(part * part, axis=1, keepdims=True)
+        for k in range(0, width, lanes):
+            part = chunk_ref[i, :, k : k + lanes].astype(jnp.float32)
+            total = total + part * part
+    total = jnp.sum(total, axis=1, keepdims=True)
     scale = lax.rsqrt(total * (1.0 / features) + 1e-05)
-    for i in parts:
-        part = (chunk_ref[i].astype(jnp.float32) * scale).astype(jnp.bfloat16)
-        block_ref[i] = part.T.reshape(nxc, rows, tokens)
+    scale = jnp.broadcast_to(scale, (tokens, lanes)).T[:1]
+    one = (
+        lax.broadcasted_iota(jnp.int32, (step, step), 0) == lax.broadcasted_iota(jnp.int32, (step, step), 1)
+    ).astype(jnp.bfloat16)
+    for i in parts:
+        turned = [
+            lax.dot_general(
+                one,
+                chunk_ref[i, :, k : k + step],
+                (((1,), (1,)), ((), ())),
+                preferred_element_type=jnp.float32,
+            )
+            for k in range(0, width, step)
+        ]
+        turned = (jnp.concatenate(turned, axis=0) * scale).astype(jnp.bfloat16)
+        block_ref[i] = turned.reshape(nxc, rows, tokens)
         leave[i].start()
     for copy in leave:
         copy.wait()
@@ -76,6 +91,27 @@
             flops=8 * activations.size, bytes_accessed=4 * activations.size, transcendentals=0
         ),
     )(activations)
+
+
+def add_kernel(kept_ref, came_ref, out_ref, block_ref, sems):
+    leave = [pltpu.make_async_copy(block_ref.at[i], out_ref.at[i], sems.at[i]) for i in range(out_ref.shape[0])]
+    for i, copy in enumerate(leave):
+        block_ref[i] = (kept_ref[i] + came_ref[i].astype(jnp.float32)).astype(block_ref.dtype)
+        copy.start()
+    for copy in leave:
+        copy.wait()
+
+
+def add_blocks(kept, came):
+    return pl.pallas_call(
+        add_kernel,
+        out_shape=jax.ShapeDtypeStruct(came.shape, came.dtype),
+        in_specs=[VMEM, VMEM],
+        out_specs=pl.BlockSpec(memory_space=pltpu.HBM),
+        scratch_shapes=[pltpu.VMEM(came.shape, came.dtype), pltpu.SemaphoreType.DMA((came.shape[0],))],
+        compiler_params=pltpu.CompilerParams(vmem_limit_bytes=16 * 2**20),
+        cost_estimate=pl.CostEstimate(flops=came.size, bytes_accessed=8 * came.size, transcendentals=0),
+    )(kept, came)
 
 
 def on_device(
@@ -177,8 +213,8 @@
 
     send = jnp.einsum("sft,fn->stn", theirs, low, preferred_element_type=f32).astype(bf16)
     part = jnp.einsum("sft,fn->stn", mine, low, preferred_element_type=f32)
-    part = lax.optimization_barrier(part) + swap(send, "c").astype(f32)
-    part, delta = lax.optimization_barrier((part.astype(bf16), delta))
+    part = add_blocks(part, swap(send, "c"))
+    part, delta = lax.optimization_barrier((part, delta))
     arrived = swap(delta, "r", 1)
     part, arrived = lax.optimization_barrier((exchange(part, "x"), arrived))
     delta = delta + arrived
@@ -203,7 +239,8 @@
     grad = jnp.sum(grad.astype(f32), axis=0)
     sent = lax.dynamic_index_in_dim(grad, 1 - z, 0, False).astype(bf16)
     kept = lax.dynamic_index_in_dim(grad, z, 0, False)
-    gradient = kept + swap(sent, "z").astype(f32)
+    came = lax.dynamic_index_in_dim(lax.all_gather(sent, "z"), 1 - z, 0, False)
+    gradient = kept + came.astype(f32)
 
     new_first = 0.9 * first_moment[0] + 0.1 * gradient
     new_second = 0.95 * second_moment[0] + 0.05 * gradient * gradient

time: 123 us -> 122 us (level)
  blocking collectives: 31.5 us -> 53.7 us
  starting transfers between devices: 49.2 us -> 33.6 us
  waiting for transfers between devices: 28.9 us -> 21.8 us
  other arithmetic: 3.88 us -> 1.81 us
    all_gather x0 -> x1, blocking collectives: none -> 22.2 us  [on_device(): came = lax.dynamic_index_in_dim(lax.all_gather(sent, 'z'), 1 - z, 0, False)]
    ppermute x6 -> x5, starting transfers between devices: 31.8 us -> 16.2 us  [swap(): return lax.ppermute(block, axis, [(i, i ^ distance) for i in range(size)])]
    ppermute x6 -> x5, waiting for transfers between devices: 21.7 us -> 14.6 us  [swap(): return lax.ppermute(block, axis, [(i, i ^ distance) for i in range(size)])]
    convert_element_type x1 -> x0, other arithmetic: 2.01 us -> none  [on_device(): part, delta = lax.optimization_barrier((part.astype(bf16), delta))]
  transfers between devices with their start and end apart: 10 -> 9, of which waited for: 9 -> 8; matrix products, arithmetic and copies ran while one was open for 2% -> 1% of each run, Pallas kernels for 0% -> 0%
where the time goes in v3:
time: 122 us
  blocking collectives  53.7 us (44%)
  starting transfers between devices  33.6 us (28%)
  waiting for transfers between devices  21.8 us (18%)
  Pallas kernels  4.12 us (3%)
  matrix products  4.06 us (3%)
  other arithmetic  1.81 us (1%)
  between operations  1.46 us (1%)
    all_gather x1, blocking collectives, on_device(): came = lax.dynamic_index_in_dim(lax.all_gather(sent, 'z'), 1 - z, 0, False)  22.2 us
    all_gather x1, blocking collectives, on_device(): low = lax.all_gather(master.astype(bf16), 'z')  18.6 us
    all_to_all x4, starting transfers between devices, exchange(): return lax.all_to_all(blocks, axes, split_axis=0, concat_axis=0, tiled=True)  17.4 us
    ppermute x5, starting transfers between devices, swap(): return lax.ppermute(block, axis, [(i, i ^ distance) for i in range(size)])  16.2 us
    ppermute x5, waiting for transfers between devices, swap(): return lax.ppermute(block, axis, [(i, i ^ distance) for i in range(size)])  14.6 us
    all_gather x1, blocking collectives, on_device(): low = lax.all_gather(low, 'y').reshape(group, columns)  12.9 us
    all_to_all x4, waiting for transfers between devices, exchange(): return lax.all_to_all(blocks, axes, split_axis=0, concat_axis=0, tiled=True)  7.23 us
    pallas_call x1, Pallas kernels, normed_blocks(): pl.pallas_call(functools.partial(norm_kernel, sizes), out_shape=jax.Shape...  3.27 us
  transfers between devices with their start and end apart: 9, of which 8 were waited for; matrix products, arithmetic and copies ran while one was open for 1% of the time, Pallas kernels for 0%

profile of v3, /device:TPU:33, one launch (start us, length us, event | category | flops | bytes accessed | tf_op | source)
XLA Modules:
  0.0 121.5 jit_solution(12008279376154453398)
XLA Ops:
  0.6 3.3 %shard_map.128 = bf16[8,4,2,96,128]{4,3,2,1,0:T(8,128)(2,1)} custom-call(bf16[128,6144]{1,0:T(8,128)(2,1)} %act_ref.1), custom_call_target="tpu_custom_call" | custom-call | flops 6291456 | bytes 3145728 | tf_op jit(solution)/shard_map/pallas_call | solution.py:161
  3.9 5.1 %all-to-all-start = ((bf16[8,768,128]{2,1,0:T(8,128)(2,1)}), bf16[8,768,128]{2,1,0:T(8,128)(2,1)S(1)}, u32[]{:S(2)}, u32[]{:S(2)}) async-start(bf16[8,768,128]{2,1,0:T(8,128)(2,1)} %bitcast.48), calls=%async_computation | async-start | bytes 3145728 | tf_op jit(solution)/shard_map/all_to_all | solution.py:23
  9.1 18.6 %all_gather.14 = bf16[2,96,512]{2,1,0:T(8,128)(2,1)S(1)} all-gather(bf16[1,96,512]{2,1,0:T(8,128)(2,1)S(1)} %convert_element_type.35), channel_id=1, replica_groups=mesh['r'=8,'z'=2,'y'=4,'x'=4,'c'=2] {'z'}, dimensions={0}, use_global_device_ids=true | all-gather | bytes 294912 | tf_op jit(solution)/shard_map/all_gather | solution.py:204
  27.7 12.9 %all-gather = bf16[8,96,512]{2,1,0:T(8,128)(2,1)S(1)} all-gather(bf16[2,96,512]{2,1,0:T(8,128)(2,1)S(1)} %all_gather.14), channel_id=2, replica_groups=mesh['r'=8,'z'=2,'y'=4,'x'=4,'c'=2] {'y'}, dimensions={0}, use_global_device_ids=true | all-gather | bytes 983040 | tf_op jit(solution)/shard_map/all_gather | solution.py:205
  40.6 1.4 %convolution_convert_fusion = bf16[4,128,512]{2,1,0:T(8,128)(2,1)} fusion(bf16[768,512,1]{1,0,2:T(8,128)(2,1)S(1)} %bitcast.46, bf16[4,2,768,128]{3,2,1,0:T(8,128)(2,1)S(1)} %bitcast.42, s32[]{:T(128)S(6)} %select_n.23), kind=kOutput, calls=%fused_computation.3 | convolution fusion | flops 402915328 | bytes 2097156 | tf_op jit(solution)/shard_map/sft,fn->stn/dot_general | solution.py:214
  42.0 3.8 %collective-permute-start = (bf16[4,128,512]{2,1,0:T(8,128)(2,1)}, bf16[4,128,512]{2,1,0:T(8,128)(2,1)S(1)}, u32[]{:S(2)}, u32[]{:S(2)}) collective-permute-start(bf16[4,128,512]{2,1,0:T(8,128)(2,1)} %convolution_convert_fusion), channel_id=1, source_target_pairs={{0,1},{1,0},{2,3},{3,2},{4,5},{5,4},{6,7},{7,6},{8,9},{9,8},{10,11... | collective-permute-start | bytes 1572872 | tf_op jit(solution)/shard_map/ppermute | solution.py:19
  47.6 0.9 shard_map.129
  48.4 4.3 %all-to-all-start.1 = ((bf16[4,128,512]{2,1,0:T(8,128)(2,1)}), bf16[4,128,512]{2,1,0:T(8,128)(2,1)S(1)}, u32[]{:S(2)}, u32[]{:S(2)}) async-start(bf16[4,128,512]{2,1,0:T(8,128)(2,1)} %shard_map.129), calls=%async_computation.1 | async-start | bytes 1048576 | tf_op jit(solution)/shard_map/all_to_all | solution.py:23
  52.7 1.9 %collective-permute-start.1 = (f32[96,128]{1,0:T(8,128)S(1)}, f32[96,128]{1,0:T(8,128)S(1)}, u32[]{:S(2)}, u32[]{:S(2)}) collective-permute-start(f32[96,128]{1,0:T(8,128)S(1)} %bitcast_subtract_fusion), channel_id=1, source_target_pairs={{0,64},{64,0},{128,192},{192,128},{256,320},{320,256},{384,448},{4... | collective-permute-start | bytes 147464 | tf_op jit(solution)/shard_map/ppermute | solution.py:19
  54.6 3.2 %collective-permute-done.1 = f32[96,128]{1,0:T(8,128)S(1)} collective-permute-done((f32[96,128]{1,0:T(8,128)S(1)}, f32[96,128]{1,0:T(8,128)S(1)}, u32[]{:S(2)}, u32[]{:S(2)}) %collective-permute-start.1) | collective-permute-done | bytes 49184 | tf_op jit(solution)/shard_map/ppermute | solution.py:19
  57.8 3.8 %all-to-all-done.1 = bf16[4,128,512]{2,1,0:T(8,128)(2,1)S(1)} async-done(((bf16[4,128,512]{2,1,0:T(8,128)(2,1)}), bf16[4,128,512]{2,1,0:T(8,128)(2,1)S(1)}, u32[]{:S(2)}, u32[]{:S(2)}) %all-to-all-start.1) | async-done | bytes 524320 | tf_op jit(solution)/shard_map/all_to_all | solution.py:23
  62.6 3.5 %all-to-all-start.2 = ((bf16[4,128,512]{2,1,0:T(8,128)(2,1)}), bf16[4,128,512]{2,1,0:T(8,128)(2,1)S(1)}, u32[]{:S(2)}, u32[]{:S(2)}) async-start(bf16[4,128,512]{2,1,0:T(8,128)(2,1)} %broadcast_in_dim.2), calls=%async_computation.2 | async-start | bytes 1048576 | tf_op jit(solution)/shard_map/all_to_all | solution.py:23
  66.1 1.9 %collective-permute-start.2 = (f32[96,128]{1,0:T(8,128)S(1)}, f32[96,128]{1,0:T(8,128)S(1)}, u32[]{:S(2)}, u32[]{:S(2)}) collective-permute-start(f32[96,128]{1,0:T(8,128)S(1)} %add.72), channel_id=1, source_target_pairs={{0,128},{64,192},{128,0},{192,64},{256,384},{320,448},{384,256},{4... | collective-permute-start | bytes 147464 | tf_op jit(solution)/shard_map/ppermute | solution.py:19
  68.0 3.8 %collective-permute-done.2 = f32[96,128]{1,0:T(8,128)S(1)} collective-permute-done((f32[96,128]{1,0:T(8,128)S(1)}, f32[96,128]{1,0:T(8,128)S(1)}, u32[]{:S(2)}, u32[]{:S(2)}) %collective-permute-start.2) | collective-permute-done | bytes 49184 | tf_op jit(solution)/shard_map/ppermute | solution.py:19
  71.8 1.9 %all-to-all-done.2 = bf16[4,128,512]{2,1,0:T(8,128)(2,1)S(1)} async-done(((bf16[4,128,512]{2,1,0:T(8,128)(2,1)}), bf16[4,128,512]{2,1,0:T(8,128)(2,1)S(1)}, u32[]{:S(2)}, u32[]{:S(2)}) %all-to-all-start.2) | async-done | bytes 524320 | tf_op jit(solution)/shard_map/all_to_all | solution.py:23
  73.8 4.6 %collective-permute-start.3 = (bf16[4,128,512]{2,1,0:T(8,128)(2,1)S(1)}, bf16[4,128,512]{2,1,0:T(8,128)(2,1)S(1)}, u32[]{:S(2)}, u32[]{:S(2)}) collective-permute-start(bf16[4,128,512]{2,1,0:T(8,128)(2,1)S(1)} %all-to-all-done.2), channel_id=1, source_target_pairs={{0,1},{1,0},{2,3},{3,2},{4,5},{5,4},{6,7},{7,6},{8,9},{9,8},{10,11... | collective-permute-start | bytes 1572872 | tf_op jit(solution)/shard_map/ppermute | solution.py:19
  79.0 0.9 collective-permute-done.3
  79.9 1.5 %fusion = bf16[768,512]{1,0:T(8,128)(2,1)} fusion(f32[768,512,1]{1,0,2:T(8,128)S(1)} %fusion.3, bf16[4,128,512]{2,1,0:T(8,128)(2,1)S(1)} %collective-permute-done.3, bf16[4,2,768,128]{3,2,1,0:T(8,128)(2,1)S(1)} %bitcast.45, s32[]{:T(128)S(6)} %select_n.23), kind=kOutput, calls=%fused_computation.1 | convolution fusion | flops 403439616 | bytes 3670020 | tf_op jit(solution)/shard_map/sft,stn->fn/dot_general | solution.py:232
  81.4 4.5 %all-to-all-start.3 = ((bf16[4,2,96,512]{3,2,1,0:T(8,128)(2,1)}), bf16[4,2,96,512]{3,2,1,0:T(8,128)(2,1)S(1)}, u32[]{:S(2)}, u32[]{:S(2)}) async-start(bf16[4,2,96,512]{3,2,1,0:T(8,128)(2,1)} %bitcast.12), calls=%async_computation.3 | async-start | bytes 1572864 | tf_op jit(solution)/shard_map/all_to_all | solution.py:23
  85.9 4.0 %collective-permute-start.4 = (f32[96,128]{1,0:T(8,128)S(1)}, f32[96,128]{1,0:T(8,128)S(1)}, u32[]{:S(2)}, u32[]{:S(2)}) collective-permute-start(f32[96,128]{1,0:T(8,128)S(1)} %add.73), channel_id=1, source_target_pairs={{0,256},{64,320},{128,384},{192,448},{256,0},{320,64},{384,128},{4... | collective-permute-start | bytes 147464 | tf_op jit(solution)/shard_map/ppermute | solution.py:19
  89.9 6.2 %collective-permute-done.4 = f32[96,128]{1,0:T(8,128)S(1)} collective-permute-done((f32[96,128]{1,0:T(8,128)S(1)}, f32[96,128]{1,0:T(8,128)S(1)}, u32[]{:S(2)}, u32[]{:S(2)}) %collective-permute-start.4) | collective-permute-done | bytes 49184 | tf_op jit(solution)/shard_map/ppermute | solution.py:19
  96.1 1.5 %all-to-all-done.3 = bf16[4,2,96,512]{3,2,1,0:T(8,128)(2,1)S(1)} async-done(((bf16[4,2,96,512]{3,2,1,0:T(8,128)(2,1)}), bf16[4,2,96,512]{3,2,1,0:T(8,128)(2,1)S(1)}, u32[]{:S(2)}, u32[]{:S(2)}) %all-to-all-start.3) | async-done | bytes 786464 | tf_op jit(solution)/shard_map/all_to_all | solution.py:23
  97.8 22.2 %all_gather.17 = bf16[2,96,512]{2,1,0:T(8,128)(2,1)S(1)} all-gather(bf16[1,96,512]{2,1,0:T(8,128)(2,1)S(1)} %dynamic-slice_convert_fusion), channel_id=1, replica_groups=mesh['r'=8,'z'=2,'y'=4,'x'=4,'c'=2] {'z'}, dimensions={0}, use_global_device_ids=true | all-gather | bytes 294912 | tf_op jit(solution)/shard_map/all_gather | solution.py:242
  120.6 0.9 multiply_subtract_fusion
  (28 shorter events, 3.4 us)
Async XLA Ops:
  3.9 5.1 %copy-start = (f32[1,96,512]{2,1,0:T(8,128)S(1)}, f32[1,96,512]{2,1,0:T(8,128)}, u32[]{:S(2)}) copy-start(f32[1,96,512]{2,1,0:T(8,128)} %param.11) | copy-start | bytes 589828
  3.9 36.7 %all-to-all-start = ((bf16[8,768,128]{2,1,0:T(8,128)(2,1)}), bf16[8,768,128]{2,1,0:T(8,128)(2,1)S(1)}, u32[]{:S(2)}, u32[]{:S(2)}) async-start(bf16[8,768,128]{2,1,0:T(8,128)(2,1)} %bitcast.48), calls=%async_computation | async-start | bytes 3145728 | tf_op jit(solution)/shard_map/all_to_all | solution.py:23
  27.7 18.8 %copy-start.4 = (f32[2,96,128]{2,1,0:T(8,128)S(1)}, f32[2,96,128]{2,1,0:T(8,128)}, u32[]{:S(2)}) copy-start(f32[2,96,128]{2,1,0:T(8,128)} %param.15) | copy-start | bytes 294916
  27.7 18.8 %copy-start.6 = (f32[1,2,96,128]{3,2,1,0:T(8,128)S(1)}, f32[1,2,96,128]{3,2,1,0:T(8,128)}, u32[]{:S(2)}) copy-start(f32[1,2,96,128]{3,2,1,0:T(8,128)} %param.14) | copy-start | bytes 294916
  42.0 5.5 %collective-permute-start = (bf16[4,128,512]{2,1,0:T(8,128)(2,1)}, bf16[4,128,512]{2,1,0:T(8,128)(2,1)S(1)}, u32[]{:S(2)}, u32[]{:S(2)}) collective-permute-start(bf16[4,128,512]{2,1,0:T(8,128)(2,1)} %convolution_convert_fusion), channel_id=1, source_target_pairs={{0,1},{1,0},{2,3},{3,2},{4,5},{5,4},{6,7},{7,6},{8,9},{9,8},{10,11... | collective-permute-start | bytes 1572872 | tf_op jit(solution)/shard_map/ppermute | solution.py:19
  47.1 14.6 %copy-start.3 = (bf16[128,512]{1,0:T(8,128)(2,1)S(1)}, bf16[128,512]{1,0:T(8,128)(2,1)}, u32[]{:S(2)}) copy-start(bf16[128,512]{1,0:T(8,128)(2,1)} %param.10) | copy-start | bytes 393220
  48.4 13.2 %all-to-all-start.1 = ((bf16[4,128,512]{2,1,0:T(8,128)(2,1)}), bf16[4,128,512]{2,1,0:T(8,128)(2,1)S(1)}, u32[]{:S(2)}, u32[]{:S(2)}) async-start(bf16[4,128,512]{2,1,0:T(8,128)(2,1)} %shard_map.129), calls=%async_computation.1 | async-start | bytes 1048576 | tf_op jit(solution)/shard_map/all_to_all | solution.py:23
  52.7 5.1 %collective-permute-start.1 = (f32[96,128]{1,0:T(8,128)S(1)}, f32[96,128]{1,0:T(8,128)S(1)}, u32[]{:S(2)}, u32[]{:S(2)}) collective-permute-start(f32[96,128]{1,0:T(8,128)S(1)} %bitcast_subtract_fusion), channel_id=1, source_target_pairs={{0,64},{64,0},{128,192},{192,128},{256,320},{320,256},{384,448},{4... | collective-permute-start | bytes 147464 | tf_op jit(solution)/shard_map/ppermute | solution.py:19
  62.6 11.1 %all-to-all-start.2 = ((bf16[4,128,512]{2,1,0:T(8,128)(2,1)}), bf16[4,128,512]{2,1,0:T(8,128)(2,1)S(1)}, u32[]{:S(2)}, u32[]{:S(2)}) async-start(bf16[4,128,512]{2,1,0:T(8,128)(2,1)} %broadcast_in_dim.2), calls=%async_computation.2 | async-start | bytes 1048576 | tf_op jit(solution)/shard_map/all_to_all | solution.py:23
  66.1 5.7 %collective-permute-start.2 = (f32[96,128]{1,0:T(8,128)S(1)}, f32[96,128]{1,0:T(8,128)S(1)}, u32[]{:S(2)}, u32[]{:S(2)}) collective-permute-start(f32[96,128]{1,0:T(8,128)S(1)} %add.72), channel_id=1, source_target_pairs={{0,128},{64,192},{128,0},{192,64},{256,384},{320,448},{384,256},{4... | collective-permute-start | bytes 147464 | tf_op jit(solution)/shard_map/ppermute | solution.py:19
  73.8 6.2 %collective-permute-start.3 = (bf16[4,128,512]{2,1,0:T(8,128)(2,1)S(1)}, bf16[4,128,512]{2,1,0:T(8,128)(2,1)S(1)}, u32[]{:S(2)}, u32[]{:S(2)}) collective-permute-start(bf16[4,128,512]{2,1,0:T(8,128)(2,1)S(1)} %all-to-all-done.2), channel_id=1, source_target_pairs={{0,1},{1,0},{2,3},{3,2},{4,5},{5,4},{6,7},{7,6},{8,9},{9,8},{10,11... | collective-permute-start | bytes 1572872 | tf_op jit(solution)/shard_map/ppermute | solution.py:19
  81.4 38.6 %copy-start.5 = (f32[2,96,128]{2,1,0:T(8,128)S(1)}, f32[2,96,128]{2,1,0:T(8,128)}, u32[]{:S(2)}) copy-start(f32[2,96,128]{2,1,0:T(8,128)} %param.16) | copy-start | bytes 294916
  81.4 39.2 %copy-start.1 = (f32[1,96,512]{2,1,0:T(8,128)S(1)}, f32[1,96,512]{2,1,0:T(8,128)}, u32[]{:S(2)}) copy-start(f32[1,96,512]{2,1,0:T(8,128)} %param.13) | copy-start | bytes 589828
  81.4 39.2 %copy-start.2 = (f32[1,96,512]{2,1,0:T(8,128)S(1)}, f32[1,96,512]{2,1,0:T(8,128)}, u32[]{:S(2)}) copy-start(f32[1,96,512]{2,1,0:T(8,128)} %param.12) | copy-start | bytes 589828
  81.4 16.2 %all-to-all-start.3 = ((bf16[4,2,96,512]{3,2,1,0:T(8,128)(2,1)}), bf16[4,2,96,512]{3,2,1,0:T(8,128)(2,1)S(1)}, u32[]{:S(2)}, u32[]{:S(2)}) async-start(bf16[4,2,96,512]{3,2,1,0:T(8,128)(2,1)} %bitcast.12), calls=%async_computation.3 | async-start | bytes 1572864 | tf_op jit(solution)/shard_map/all_to_all | solution.py:23
  85.9 10.2 %collective-permute-start.4 = (f32[96,128]{1,0:T(8,128)S(1)}, f32[96,128]{1,0:T(8,128)S(1)}, u32[]{:S(2)}, u32[]{:S(2)}) collective-permute-start(f32[96,128]{1,0:T(8,128)S(1)} %add.73), channel_id=1, source_target_pairs={{0,256},{64,320},{128,384},{192,448},{256,0},{320,64},{384,128},{4... | collective-permute-start | bytes 147464 | tf_op jit(solution)/shard_map/ppermute | solution.py:19

commit v4 on v3

--- a/solution.py
+++ b/solution.py
@@ -234,8 +234,10 @@
     delta, grad = lax.optimization_barrier((delta, grad))
     arrived = swap(delta, "r", 4)
     grad = exchange(grad, "y")
-    grad, arrived = lax.optimization_barrier((grad, arrived))
-    delta = delta + arrived
+    mean_delta = (delta + arrived) / lax.axis_size("r")
+    new_momentum = 0.9 * moment_part + mean_delta
+    new_global = global_part - 0.7 * (mean_delta + 0.9 * new_momentum)
+    grad, new_global, new_momentum = lax.optimization_barrier((grad, new_global, new_momentum))
     grad = jnp.sum(grad.astype(f32), axis=0)
     sent = lax.dynamic_index_in_dim(grad, 1 - z, 0, False).astype(bf16)
     kept = lax.dynamic_index_in_dim(grad, z, 0, False)
@@ -246,9 +248,6 @@
     new_second = 0.95 * second_moment[0] + 0.05 * gradient * gradient
     new_master = master - 0.01 * (new_first / (jnp.sqrt(new_second) + 1e-08) + 0.1 * master)
 
-    mean_delta = delta / lax.axis_size("r")
-    new_momentum = 0.9 * moment_part + mean_delta
-    new_global = global_part - 0.7 * (mean_delta + 0.9 * new_momentum)
     return (new_master[None], new_first[None], new_second[None], new_global, new_momentum)
 
 

time: 122 us -> 122 us (level)
  transfers between devices with their start and end apart: 9 -> 9, of which waited for: 8 -> 8; matrix products, arithmetic and copies ran while one was open for 1% -> 2% of each run, Pallas kernels for 0% -> 0%
where the time goes in v4:
time: 122 us; the launch traced here: 121 us
  blocking collectives  54.2 us (44%)
  starting transfers between devices  33.6 us (28%)
  waiting for transfers between devices  21.1 us (17%)
  Pallas kernels  4.12 us (3%)
  matrix products  4.06 us (3%)
  other arithmetic  1.81 us (1%)
  between operations  1.46 us (1%)
    all_gather x1, blocking collectives, on_device(): came = lax.dynamic_index_in_dim(lax.all_gather(sent, 'z'), 1 - z, 0, False)  22.7 us
    all_gather x1, blocking collectives, on_device(): low = lax.all_gather(master.astype(bf16), 'z')  18.6 us
    all_to_all x4, starting transfers between devices, exchange(): return lax.all_to_all(blocks, axes, split_axis=0, concat_axis=0, tiled=True)  17.4 us
    ppermute x5, starting transfers between devices, swap(): return lax.ppermute(block, axis, [(i, i ^ distance) for i in range(size)])  16.2 us
    ppermute x5, waiting for transfers between devices, swap(): return lax.ppermute(block, axis, [(i, i ^ distance) for i in range(size)])  14.6 us
    all_gather x1, blocking collectives, on_device(): low = lax.all_gather(low, 'y').reshape(group, columns)  12.9 us
    all_to_all x4, waiting for transfers between devices, exchange(): return lax.all_to_all(blocks, axes, split_axis=0, concat_axis=0, tiled=True)  6.58 us
    pallas_call x1, Pallas kernels, normed_blocks(): pl.pallas_call(functools.partial(norm_kernel, sizes), out_shape=jax.Shape...  3.27 us
  transfers between devices with their start and end apart: 9, of which 8 were waited for; matrix products, arithmetic and copies ran while one was open for 2% of the time, Pallas kernels for 0%

profile of v4, /device:TPU:33, one launch (start us, length us, event | category | flops | bytes accessed | tf_op | source)
XLA Modules:
  0.0 121.3 jit_solution(9504921178995612842)
XLA Ops:
  0.6 3.3 %shard_map.128 = bf16[8,4,2,96,128]{4,3,2,1,0:T(8,128)(2,1)} custom-call(bf16[128,6144]{1,0:T(8,128)(2,1)} %act_ref.1), custom_call_target="tpu_custom_call" | custom-call | flops 6291456 | bytes 3145728 | tf_op jit(solution)/shard_map/pallas_call | solution.py:161
  3.9 5.1 %all-to-all-start = ((bf16[8,768,128]{2,1,0:T(8,128)(2,1)}), bf16[8,768,128]{2,1,0:T(8,128)(2,1)S(1)}, u32[]{:S(2)}, u32[]{:S(2)}) async-start(bf16[8,768,128]{2,1,0:T(8,128)(2,1)} %bitcast.49), calls=%async_computation | async-start | bytes 3145728 | tf_op jit(solution)/shard_map/all_to_all | solution.py:23
  9.1 18.6 %all_gather.14 = bf16[2,96,512]{2,1,0:T(8,128)(2,1)S(1)} all-gather(bf16[1,96,512]{2,1,0:T(8,128)(2,1)S(1)} %convert_element_type.35), channel_id=1, replica_groups=mesh['r'=8,'z'=2,'y'=4,'x'=4,'c'=2] {'z'}, dimensions={0}, use_global_device_ids=true | all-gather | bytes 294912 | tf_op jit(solution)/shard_map/all_gather | solution.py:204
  27.7 12.9 %all-gather = bf16[8,96,512]{2,1,0:T(8,128)(2,1)S(1)} all-gather(bf16[2,96,512]{2,1,0:T(8,128)(2,1)S(1)} %all_gather.14), channel_id=2, replica_groups=mesh['r'=8,'z'=2,'y'=4,'x'=4,'c'=2] {'y'}, dimensions={0}, use_global_device_ids=true | all-gather | bytes 983040 | tf_op jit(solution)/shard_map/all_gather | solution.py:205
  40.6 1.4 %convolution_convert_fusion = bf16[4,128,512]{2,1,0:T(8,128)(2,1)} fusion(bf16[768,512,1]{1,0,2:T(8,128)(2,1)S(1)} %bitcast.47, bf16[4,2,768,128]{3,2,1,0:T(8,128)(2,1)S(1)} %bitcast.43, s32[]{:T(128)S(6)} %select_n.23), kind=kOutput, calls=%fused_computation.3 | convolution fusion | flops 402915328 | bytes 2097156 | tf_op jit(solution)/shard_map/sft,fn->stn/dot_general | solution.py:214
  42.0 3.8 %collective-permute-start = (bf16[4,128,512]{2,1,0:T(8,128)(2,1)}, bf16[4,128,512]{2,1,0:T(8,128)(2,1)S(1)}, u32[]{:S(2)}, u32[]{:S(2)}) collective-permute-start(bf16[4,128,512]{2,1,0:T(8,128)(2,1)} %convolution_convert_fusion), channel_id=1, source_target_pairs={{0,1},{1,0},{2,3},{3,2},{4,5},{5,4},{6,7},{7,6},{8,9},{9,8},{10,11... | collective-permute-start | bytes 1572872 | tf_op jit(solution)/shard_map/ppermute | solution.py:19
  47.6 0.9 shard_map.129
  48.4 4.3 %all-to-all-start.1 = ((bf16[4,128,512]{2,1,0:T(8,128)(2,1)}), bf16[4,128,512]{2,1,0:T(8,128)(2,1)S(1)}, u32[]{:S(2)}, u32[]{:S(2)}) async-start(bf16[4,128,512]{2,1,0:T(8,128)(2,1)} %shard_map.129), calls=%async_computation.1 | async-start | bytes 1048576 | tf_op jit(solution)/shard_map/all_to_all | solution.py:23
  52.7 1.9 %collective-permute-start.1 = (f32[96,128]{1,0:T(8,128)S(1)}, f32[96,128]{1,0:T(8,128)S(1)}, u32[]{:S(2)}, u32[]{:S(2)}) collective-permute-start(f32[96,128]{1,0:T(8,128)S(1)} %bitcast_subtract_fusion), channel_id=1, source_target_pairs={{0,64},{64,0},{128,192},{192,128},{256,320},{320,256},{384,448},{4... | collective-permute-start | bytes 147464 | tf_op jit(solution)/shard_map/ppermute | solution.py:19
  54.6 3.2 %collective-permute-done.1 = f32[96,128]{1,0:T(8,128)S(1)} collective-permute-done((f32[96,128]{1,0:T(8,128)S(1)}, f32[96,128]{1,0:T(8,128)S(1)}, u32[]{:S(2)}, u32[]{:S(2)}) %collective-permute-start.1) | collective-permute-done | bytes 49184 | tf_op jit(solution)/shard_map/ppermute | solution.py:19
  57.8 3.8 %all-to-all-done.1 = bf16[4,128,512]{2,1,0:T(8,128)(2,1)S(1)} async-done(((bf16[4,128,512]{2,1,0:T(8,128)(2,1)}), bf16[4,128,512]{2,1,0:T(8,128)(2,1)S(1)}, u32[]{:S(2)}, u32[]{:S(2)}) %all-to-all-start.1) | async-done | bytes 524320 | tf_op jit(solution)/shard_map/all_to_all | solution.py:23
  62.6 3.5 %all-to-all-start.2 = ((bf16[4,128,512]{2,1,0:T(8,128)(2,1)}), bf16[4,128,512]{2,1,0:T(8,128)(2,1)S(1)}, u32[]{:S(2)}, u32[]{:S(2)}) async-start(bf16[4,128,512]{2,1,0:T(8,128)(2,1)} %broadcast_in_dim.2), calls=%async_computation.2 | async-start | bytes 1048576 | tf_op jit(solution)/shard_map/all_to_all | solution.py:23
  66.1 1.9 %collective-permute-start.2 = (f32[96,128]{1,0:T(8,128)S(1)}, f32[96,128]{1,0:T(8,128)S(1)}, u32[]{:S(2)}, u32[]{:S(2)}) collective-permute-start(f32[96,128]{1,0:T(8,128)S(1)} %add.72), channel_id=1, source_target_pairs={{0,128},{64,192},{128,0},{192,64},{256,384},{320,448},{384,256},{4... | collective-permute-start | bytes 147464 | tf_op jit(solution)/shard_map/ppermute | solution.py:19
  68.0 3.8 %collective-permute-done.2 = f32[96,128]{1,0:T(8,128)S(1)} collective-permute-done((f32[96,128]{1,0:T(8,128)S(1)}, f32[96,128]{1,0:T(8,128)S(1)}, u32[]{:S(2)}, u32[]{:S(2)}) %collective-permute-start.2) | collective-permute-done | bytes 49184 | tf_op jit(solution)/shard_map/ppermute | solution.py:19
  71.8 1.9 %all-to-all-done.2 = bf16[4,128,512]{2,1,0:T(8,128)(2,1)S(1)} async-done(((bf16[4,128,512]{2,1,0:T(8,128)(2,1)}), bf16[4,128,512]{2,1,0:T(8,128)(2,1)S(1)}, u32[]{:S(2)}, u32[]{:S(2)}) %all-to-all-start.2) | async-done | bytes 524320 | tf_op jit(solution)/shard_map/all_to_all | solution.py:23
  73.8 4.6 %collective-permute-start.3 = (bf16[4,128,512]{2,1,0:T(8,128)(2,1)S(1)}, bf16[4,128,512]{2,1,0:T(8,128)(2,1)S(1)}, u32[]{:S(2)}, u32[]{:S(2)}) collective-permute-start(bf16[4,128,512]{2,1,0:T(8,128)(2,1)S(1)} %all-to-all-done.2), channel_id=1, source_target_pairs={{0,1},{1,0},{2,3},{3,2},{4,5},{5,4},{6,7},{7,6},{8,9},{9,8},{10,11... | collective-permute-start | bytes 1572872 | tf_op jit(solution)/shard_map/ppermute | solution.py:19
  79.0 0.9 collective-permute-done.3
  79.9 1.5 %fusion = bf16[768,512]{1,0:T(8,128)(2,1)} fusion(f32[768,512,1]{1,0,2:T(8,128)S(1)} %fusion.3, bf16[4,128,512]{2,1,0:T(8,128)(2,1)S(1)} %collective-permute-done.3, bf16[4,2,768,128]{3,2,1,0:T(8,128)(2,1)S(1)} %bitcast.46, s32[]{:T(128)S(6)} %select_n.23), kind=kOutput, calls=%fused_computation.1 | convolution fusion | flops 403439616 | bytes 3670020 | tf_op jit(solution)/shard_map/sft,stn->fn/dot_general | solution.py:232
  81.4 4.5 %all-to-all-start.3 = ((bf16[4,2,96,512]{3,2,1,0:T(8,128)(2,1)}), bf16[4,2,96,512]{3,2,1,0:T(8,128)(2,1)S(1)}, u32[]{:S(2)}, u32[]{:S(2)}) async-start(bf16[4,2,96,512]{3,2,1,0:T(8,128)(2,1)} %bitcast.12), calls=%async_computation.3 | async-start | bytes 1572864 | tf_op jit(solution)/shard_map/all_to_all | solution.py:23
  85.9 4.0 %collective-permute-start.4 = (f32[96,128]{1,0:T(8,128)S(1)}, f32[96,128]{1,0:T(8,128)S(1)}, u32[]{:S(2)}, u32[]{:S(2)}) collective-permute-start(f32[96,128]{1,0:T(8,128)S(1)} %add.73), channel_id=1, source_target_pairs={{0,256},{64,320},{128,384},{192,448},{256,0},{320,64},{384,128},{4... | collective-permute-start | bytes 147464 | tf_op jit(solution)/shard_map/ppermute | solution.py:19
  89.9 6.2 %collective-permute-done.4 = f32[96,128]{1,0:T(8,128)S(1)} collective-permute-done((f32[96,128]{1,0:T(8,128)S(1)}, f32[96,128]{1,0:T(8,128)S(1)}, u32[]{:S(2)}, u32[]{:S(2)}) %collective-permute-start.4) | collective-permute-done | bytes 49184 | tf_op jit(solution)/shard_map/ppermute | solution.py:19
  96.7 0.9 all-to-all-done.3
  97.8 22.7 %all_gather.17 = bf16[2,96,512]{2,1,0:T(8,128)(2,1)S(1)} all-gather(bf16[1,96,512]{2,1,0:T(8,128)(2,1)S(1)} %dynamic-slice_convert_fusion), channel_id=1, replica_groups=mesh['r'=8,'z'=2,'y'=4,'x'=4,'c'=2] {'z'}, dimensions={0}, use_global_device_ids=true | all-gather | bytes 294912 | tf_op jit(solution)/shard_map/all_gather | solution.py:244
  120.4 0.9 multiply_subtract_fusion
  (28 shorter events, 3.4 us)
Async XLA Ops:
  3.9 5.1 %copy-start = (f32[1,96,512]{2,1,0:T(8,128)S(1)}, f32[1,96,512]{2,1,0:T(8,128)}, u32[]{:S(2)}) copy-start(f32[1,96,512]{2,1,0:T(8,128)} %param.11) | copy-start | bytes 589828
  3.9 36.7 %all-to-all-start = ((bf16[8,768,128]{2,1,0:T(8,128)(2,1)}), bf16[8,768,128]{2,1,0:T(8,128)(2,1)S(1)}, u32[]{:S(2)}, u32[]{:S(2)}) async-start(bf16[8,768,128]{2,1,0:T(8,128)(2,1)} %bitcast.49), calls=%async_computation | async-start | bytes 3145728 | tf_op jit(solution)/shard_map/all_to_all | solution.py:23
  27.7 18.8 %copy-start.4 = (f32[2,96,128]{2,1,0:T(8,128)S(1)}, f32[2,96,128]{2,1,0:T(8,128)}, u32[]{:S(2)}) copy-start(f32[2,96,128]{2,1,0:T(8,128)} %param.15) | copy-start | bytes 294916
  27.7 18.8 %copy-start.6 = (f32[1,2,96,128]{3,2,1,0:T(8,128)S(1)}, f32[1,2,96,128]{3,2,1,0:T(8,128)}, u32[]{:S(2)}) copy-start(f32[1,2,96,128]{3,2,1,0:T(8,128)} %param.14) | copy-start | bytes 294916
  42.0 5.5 %collective-permute-start = (bf16[4,128,512]{2,1,0:T(8,128)(2,1)}, bf16[4,128,512]{2,1,0:T(8,128)(2,1)S(1)}, u32[]{:S(2)}, u32[]{:S(2)}) collective-permute-start(bf16[4,128,512]{2,1,0:T(8,128)(2,1)} %convolution_convert_fusion), channel_id=1, source_target_pairs={{0,1},{1,0},{2,3},{3,2},{4,5},{5,4},{6,7},{7,6},{8,9},{9,8},{10,11... | collective-permute-start | bytes 1572872 | tf_op jit(solution)/shard_map/ppermute | solution.py:19
  47.1 14.6 %copy-start.3 = (bf16[128,512]{1,0:T(8,128)(2,1)S(1)}, bf16[128,512]{1,0:T(8,128)(2,1)}, u32[]{:S(2)}) copy-start(bf16[128,512]{1,0:T(8,128)(2,1)} %param.10) | copy-start | bytes 393220
  48.4 13.2 %all-to-all-start.1 = ((bf16[4,128,512]{2,1,0:T(8,128)(2,1)}), bf16[4,128,512]{2,1,0:T(8,128)(2,1)S(1)}, u32[]{:S(2)}, u32[]{:S(2)}) async-start(bf16[4,128,512]{2,1,0:T(8,128)(2,1)} %shard_map.129), calls=%async_computation.1 | async-start | bytes 1048576 | tf_op jit(solution)/shard_map/all_to_all | solution.py:23
  52.7 5.1 %collective-permute-start.1 = (f32[96,128]{1,0:T(8,128)S(1)}, f32[96,128]{1,0:T(8,128)S(1)}, u32[]{:S(2)}, u32[]{:S(2)}) collective-permute-start(f32[96,128]{1,0:T(8,128)S(1)} %bitcast_subtract_fusion), channel_id=1, source_target_pairs={{0,64},{64,0},{128,192},{192,128},{256,320},{320,256},{384,448},{4... | collective-permute-start | bytes 147464 | tf_op jit(solution)/shard_map/ppermute | solution.py:19
  62.6 11.1 %all-to-all-start.2 = ((bf16[4,128,512]{2,1,0:T(8,128)(2,1)}), bf16[4,128,512]{2,1,0:T(8,128)(2,1)S(1)}, u32[]{:S(2)}, u32[]{:S(2)}) async-start(bf16[4,128,512]{2,1,0:T(8,128)(2,1)} %broadcast_in_dim.2), calls=%async_computation.2 | async-start | bytes 1048576 | tf_op jit(solution)/shard_map/all_to_all | solution.py:23
  66.1 5.7 %collective-permute-start.2 = (f32[96,128]{1,0:T(8,128)S(1)}, f32[96,128]{1,0:T(8,128)S(1)}, u32[]{:S(2)}, u32[]{:S(2)}) collective-permute-start(f32[96,128]{1,0:T(8,128)S(1)} %add.72), channel_id=1, source_target_pairs={{0,128},{64,192},{128,0},{192,64},{256,384},{320,448},{384,256},{4... | collective-permute-start | bytes 147464 | tf_op jit(solution)/shard_map/ppermute | solution.py:19
  73.8 6.2 %collective-permute-start.3 = (bf16[4,128,512]{2,1,0:T(8,128)(2,1)S(1)}, bf16[4,128,512]{2,1,0:T(8,128)(2,1)S(1)}, u32[]{:S(2)}, u32[]{:S(2)}) collective-permute-start(bf16[4,128,512]{2,1,0:T(8,128)(2,1)S(1)} %all-to-all-done.2), channel_id=1, source_target_pairs={{0,1},{1,0},{2,3},{3,2},{4,5},{5,4},{6,7},{7,6},{8,9},{9,8},{10,11... | collective-permute-start | bytes 1572872 | tf_op jit(solution)/shard_map/ppermute | solution.py:19
  81.4 14.7 %copy-start.5 = (f32[2,96,128]{2,1,0:T(8,128)S(1)}, f32[2,96,128]{2,1,0:T(8,128)}, u32[]{:S(2)}) copy-start(f32[2,96,128]{2,1,0:T(8,128)} %param.16) | copy-start | bytes 294916
  81.4 39.0 %copy-start.1 = (f32[1,96,512]{2,1,0:T(8,128)S(1)}, f32[1,96,512]{2,1,0:T(8,128)}, u32[]{:S(2)}) copy-start(f32[1,96,512]{2,1,0:T(8,128)} %param.13) | copy-start | bytes 589828
  81.4 39.0 %copy-start.2 = (f32[1,96,512]{2,1,0:T(8,128)S(1)}, f32[1,96,512]{2,1,0:T(8,128)}, u32[]{:S(2)}) copy-start(f32[1,96,512]{2,1,0:T(8,128)} %param.12) | copy-start | bytes 589828
  81.4 16.2 %all-to-all-start.3 = ((bf16[4,2,96,512]{3,2,1,0:T(8,128)(2,1)}), bf16[4,2,96,512]{3,2,1,0:T(8,128)(2,1)S(1)}, u32[]{:S(2)}, u32[]{:S(2)}) async-start(bf16[4,2,96,512]{3,2,1,0:T(8,128)(2,1)} %bitcast.12), calls=%async_computation.3 | async-start | bytes 1572864 | tf_op jit(solution)/shard_map/all_to_all | solution.py:23
  85.9 10.2 %collective-permute-start.4 = (f32[96,128]{1,0:T(8,128)S(1)}, f32[96,128]{1,0:T(8,128)S(1)}, u32[]{:S(2)}, u32[]{:S(2)}) collective-permute-start(f32[96,128]{1,0:T(8,128)S(1)} %add.73), channel_id=1, source_target_pairs={{0,256},{64,320},{128,384},{192,448},{256,0},{320,64},{384,128},{4... | collective-permute-start | bytes 147464 | tf_op jit(solution)/shard_map/ppermute | solution.py:19

commit v5 on v4

--- a/solution.py
+++ b/solution.py
@@ -17,6 +17,12 @@
 def swap(block, axis, distance=1):
     size = lax.axis_size(axis)
     return lax.ppermute(block, axis, [(i, i ^ distance) for i in range(size)])
+
+
+def pair_sum(block, axis, distance):
+    groups = [[i, i ^ distance] for i in range(lax.axis_size(axis)) if not i & distance]
+    both = lax.all_gather(block, axis, axis_index_groups=groups)
+    return both[0] + both[1]
 
 
 def exchange(blocks, axes):
@@ -112,6 +118,26 @@
         compiler_params=pltpu.CompilerParams(vmem_limit_bytes=16 * 2**20),
         cost_estimate=pl.CostEstimate(flops=came.size, bytes_accessed=8 * came.size, transcendentals=0),
     )(kept, came)
+
+
+def cotangent_kernel(factor, part_ref, target_ref, out_ref):
+    total = part_ref[0].astype(jnp.float32)
+    for i in range(1, part_ref.shape[0]):
+        total = total + part_ref[i].astype(jnp.float32)
+    block = ((total - target_ref[...].astype(jnp.float32)) * factor).astype(out_ref.dtype)
+    for i in range(out_ref.shape[0]):
+        out_ref[i] = block
+
+
+def cotangents(factor, part, target):
+    return pl.pallas_call(
+        functools.partial(cotangent_kernel, factor),
+        out_shape=jax.ShapeDtypeStruct(part.shape, target.dtype),
+        in_specs=[VMEM, VMEM],
+        out_specs=VMEM,
+        compiler_params=pltpu.CompilerParams(vmem_limit_bytes=8 * 2**20),
+        cost_estimate=pl.CostEstimate(flops=2 * part.size, bytes_accessed=5 * part.size, transcendentals=0),
+    )(part, target)
 
 
 def on_device(
@@ -215,26 +241,19 @@
     part = jnp.einsum("sft,fn->stn", mine, low, preferred_element_type=f32)
     part = add_blocks(part, swap(send, "c"))
     part, delta = lax.optimization_barrier((part, delta))
-    arrived = swap(delta, "r", 1)
-    part, arrived = lax.optimization_barrier((exchange(part, "x"), arrived))
-    delta = delta + arrived
-    part = part.astype(f32)
+    part, delta = lax.optimization_barrier((exchange(part, "x"), pair_sum(delta, "r", 1)))
     factor = 1.0 / math.sqrt(tokens * nz * ny * nx * nc)
-    cotangent = ((jnp.sum(part, axis=0) - targets.astype(f32)) * factor).astype(bf16)
+    cotangent = cotangents(factor, part, targets)
     cotangent, delta = lax.optimization_barrier((cotangent, delta))
-    arrived = swap(delta, "r", 2)
-    near = spread(cotangent, "x")
-    near, arrived = lax.optimization_barrier((near, arrived))
-    delta = delta + arrived
+    near, delta = lax.optimization_barrier((exchange(cotangent, "x"), pair_sum(delta, "r", 2)))
     far = swap(near, "c")
 
     grad = jnp.einsum("sft,stn->fn", mine, near, preferred_element_type=f32)
     grad = grad + jnp.einsum("sft,stn->fn", theirs, far, preferred_element_type=f32)
     grad = grad.reshape(ny, nz, rows, columns).astype(bf16)
     delta, grad = lax.optimization_barrier((delta, grad))
-    arrived = swap(delta, "r", 4)
     grad = exchange(grad, "y")
-    mean_delta = (delta + arrived) / lax.axis_size("r")
+    mean_delta = pair_sum(delta, "r", 4) / lax.axis_size("r")
     new_momentum = 0.9 * moment_part + mean_delta
     new_global = global_part - 0.7 * (mean_delta + 0.9 * new_momentum)
     grad, new_global, new_momentum = lax.optimization_barrier((grad, new_global, new_momentum))

time: 122 us -> 121 us (level)
  blocking collectives: 54.2 us -> 69.9 us
  waiting for transfers between devices: 21.1 us -> 12.8 us
  starting transfers between devices: 33.6 us -> 25.8 us
    all_gather x0 -> x3, blocking collectives: none -> 16.2 us  [pair_sum(): both = lax.all_gather(block, axis, axis_index_groups=groups)]
    ppermute x5 -> x2, waiting for transfers between devices: 14.6 us -> 1.36 us  [swap(): return lax.ppermute(block, axis, [(i, i ^ distance) for i in range(size)])]
    ppermute x5 -> x2, starting transfers between devices: 16.2 us -> 8.45 us  [swap(): return lax.ppermute(block, axis, [(i, i ^ distance) for i in range(size)])]
    all_to_all x4, waiting for transfers between devices: 6.58 us -> 11.5 us  [exchange(): return lax.all_to_all(blocks, axes, split_axis=0, concat_axis=0, tiled=True)]
  transfers between devices with their start and end apart: 9 -> 6, of which waited for: 8 -> 5; matrix products, arithmetic and copies ran while one was open for 2% -> 2% of each run, Pallas kernels for 0% -> 0%
where the time goes in v5:
time: 121 us
  blocking collectives  69.9 us (58%)
  starting transfers between devices  25.8 us (21%)
  waiting for transfers between devices  12.8 us (11%)
  Pallas kernels  5.01 us (4%)
  matrix products  4.05 us (3%)
  other arithmetic  1.7 us (1%)
  between operations  1.4 us (1%)
    all_gather x1, blocking collectives, on_device(): came = lax.dynamic_index_in_dim(lax.all_gather(sent, 'z'), 1 - z, 0, False)  22.2 us
    all_gather x1, blocking collectives, on_device(): low = lax.all_gather(master.astype(bf16), 'z')  18.6 us
    all_to_all x4, starting transfers between devices, exchange(): return lax.all_to_all(blocks, axes, split_axis=0, concat_axis=0, tiled=True)  17.4 us
    all_gather x3, blocking collectives, pair_sum(): both = lax.all_gather(block, axis, axis_index_groups=groups)  16.2 us
    all_gather x1, blocking collectives, on_device(): low = lax.all_gather(low, 'y').reshape(group, columns)  12.9 us
    all_to_all x4, waiting for transfers between devices, exchange(): return lax.all_to_all(blocks, axes, split_axis=0, concat_axis=0, tiled=True)  11.5 us
    ppermute x2, starting transfers between devices, swap(): return lax.ppermute(block, axis, [(i, i ^ distance) for i in range(size)])  8.45 us
    pallas_call x1, Pallas kernels, normed_blocks(): pl.pallas_call(functools.partial(norm_kernel, sizes), out_shape=jax.Shape...  3.27 us
  transfers between devices with their start and end apart: 6, of which 5 were waited for; matrix products, arithmetic and copies ran while one was open for 2% of the time, Pallas kernels for 0%

profile of v5, /device:TPU:33, one launch (start us, length us, event | category | flops | bytes accessed | tf_op | source)
XLA Modules:
  0.0 120.8 jit_solution(11457159456404595468)
XLA Ops:
  0.6 3.3 %shard_map.128 = bf16[8,4,2,96,128]{4,3,2,1,0:T(8,128)(2,1)} custom-call(bf16[128,6144]{1,0:T(8,128)(2,1)} %act_ref.1), custom_call_target="tpu_custom_call" | custom-call | flops 6291456 | bytes 3145728 | tf_op jit(solution)/shard_map/pallas_call | solution.py:187
  3.9 5.1 %all-to-all-start = ((bf16[8,768,128]{2,1,0:T(8,128)(2,1)}), bf16[8,768,128]{2,1,0:T(8,128)(2,1)S(1)}, u32[]{:S(2)}, u32[]{:S(2)}) async-start(bf16[8,768,128]{2,1,0:T(8,128)(2,1)} %bitcast.48), calls=%async_computation | async-start | bytes 3145728 | tf_op jit(solution)/shard_map/all_to_all | solution.py:29
  9.1 18.6 %all_gather.32 = bf16[2,96,512]{2,1,0:T(8,128)(2,1)S(1)} all-gather(bf16[1,96,512]{2,1,0:T(8,128)(2,1)S(1)} %convert_element_type.26), channel_id=1, replica_groups=mesh['r'=8,'z'=2,'y'=4,'x'=4,'c'=2] {'z'}, dimensions={0}, use_global_device_ids=true | all-gather | bytes 294912 | tf_op jit(solution)/shard_map/all_gather | solution.py:230
  27.7 12.9 %all-gather = bf16[8,96,512]{2,1,0:T(8,128)(2,1)S(1)} all-gather(bf16[2,96,512]{2,1,0:T(8,128)(2,1)S(1)} %all_gather.32), channel_id=2, replica_groups=mesh['r'=8,'z'=2,'y'=4,'x'=4,'c'=2] {'y'}, dimensions={0}, use_global_device_ids=true | all-gather | bytes 983040 | tf_op jit(solution)/shard_map/all_gather | solution.py:231
  40.6 1.4 %convolution_convert_fusion = bf16[4,128,512]{2,1,0:T(8,128)(2,1)} fusion(bf16[768,512,1]{1,0,2:T(8,128)(2,1)S(1)} %bitcast.46, bf16[4,2,768,128]{3,2,1,0:T(8,128)(2,1)S(1)} %bitcast.42, s32[]{:T(128)S(6)} %select_n.23), kind=kOutput, calls=%fused_computation.3 | convolution fusion | flops 402915328 | bytes 2097156 | tf_op jit(solution)/shard_map/sft,fn->stn/dot_general | solution.py:240
  42.0 3.8 %collective-permute-start = (bf16[4,128,512]{2,1,0:T(8,128)(2,1)}, bf16[4,128,512]{2,1,0:T(8,128)(2,1)S(1)}, u32[]{:S(2)}, u32[]{:S(2)}) collective-permute-start(bf16[4,128,512]{2,1,0:T(8,128)(2,1)} %convolution_convert_fusion), channel_id=1, source_target_pairs={{0,1},{1,0},{2,3},{3,2},{4,5},{5,4},{6,7},{7,6},{8,9},{9,8},{10,11... | collective-permute-start | bytes 1572872 | tf_op jit(solution)/shard_map/ppermute | solution.py:19
  46.5 0.6 fusion.5.kept_ref
  47.6 0.9 shard_map.129
  48.4 4.3 %all-to-all-start.1 = ((bf16[4,128,512]{2,1,0:T(8,128)(2,1)}), bf16[4,128,512]{2,1,0:T(8,128)(2,1)S(1)}, u32[]{:S(2)}, u32[]{:S(2)}) async-start(bf16[4,128,512]{2,1,0:T(8,128)(2,1)} %shard_map.129), calls=%async_computation.1 | async-start | bytes 1048576 | tf_op jit(solution)/shard_map/all_to_all | solution.py:29
  52.7 3.6 %all-gather.1 = f32[192,128]{1,0:T(8,128)S(1)} all-gather(f32[96,128]{1,0:T(8,128)S(1)} %bitcast_subtract_fusion), channel_id=3, replica_groups={{0,64},{128,192},{256,320},{384,448},{1,65},{129,193},{257,321},{385,44..., dimensions={0}, use_global_device_ids=true | all-gather | bytes 147456 | tf_op jit(solution)/shard_map/all_gather | solution.py:24
  56.3 5.3 %all-to-all-done.1.part_ref = bf16[4,128,512]{2,1,0:T(8,128)(2,1)S(1)} async-done(((bf16[4,128,512]{2,1,0:T(8,128)(2,1)}), bf16[4,128,512]{2,1,0:T(8,128)(2,1)S(1)}, u32[]{:S(2)}, u32[]{:S(2)}) %all-to-all-start.1) | async-done | bytes 524320 | tf_op jit(solution)/shard_map/all_to_all | solution.py:29
  61.6 0.9 shard_map.130
  62.5 3.5 %all-to-all-start.2 = ((bf16[4,128,512]{2,1,0:T(8,128)(2,1)}), bf16[4,128,512]{2,1,0:T(8,128)(2,1)S(1)}, u32[]{:S(2)}, u32[]{:S(2)}) async-start(bf16[4,128,512]{2,1,0:T(8,128)(2,1)} %shard_map.130), calls=%async_computation.2 | async-start | bytes 1048576 | tf_op jit(solution)/shard_map/all_to_all | solution.py:29
  66.0 4.5 %all-gather.2 = f32[192,128]{1,0:T(8,128)S(1)} all-gather(f32[96,128]{1,0:T(8,128)S(1)} %slice_add_fusion.2), channel_id=4, replica_groups={{0,128},{64,192},{256,384},{320,448},{1,129},{65,193},{257,385},{321,44..., dimensions={0}, use_global_device_ids=true | all-gather | bytes 147456 | tf_op jit(solution)/shard_map/all_gather | solution.py:24
  70.5 3.1 %all-to-all-done.2 = bf16[4,128,512]{2,1,0:T(8,128)(2,1)S(1)} async-done(((bf16[4,128,512]{2,1,0:T(8,128)(2,1)}), bf16[4,128,512]{2,1,0:T(8,128)(2,1)S(1)}, u32[]{:S(2)}, u32[]{:S(2)}) %all-to-all-start.2) | async-done | bytes 524320 | tf_op jit(solution)/shard_map/all_to_all | solution.py:29
  73.7 4.6 %collective-permute-start.1 = (bf16[4,128,512]{2,1,0:T(8,128)(2,1)S(1)}, bf16[4,128,512]{2,1,0:T(8,128)(2,1)S(1)}, u32[]{:S(2)}, u32[]{:S(2)}) collective-permute-start(bf16[4,128,512]{2,1,0:T(8,128)(2,1)S(1)} %all-to-all-done.2), channel_id=1, source_target_pairs={{0,1},{1,0},{2,3},{3,2},{4,5},{5,4},{6,7},{7,6},{8,9},{9,8},{10,11... | collective-permute-start | bytes 1572872 | tf_op jit(solution)/shard_map/ppermute | solution.py:19
  78.9 0.9 collective-permute-done.1
  79.8 1.5 %fusion = bf16[768,512]{1,0:T(8,128)(2,1)} fusion(f32[768,512,1]{1,0,2:T(8,128)S(1)} %fusion.3, bf16[4,128,512]{2,1,0:T(8,128)(2,1)S(1)} %collective-permute-done.1, bf16[4,2,768,128]{3,2,1,0:T(8,128)(2,1)S(1)} %bitcast.45, s32[]{:T(128)S(6)} %select_n.23), kind=kOutput, calls=%fused_computation.1 | convolution fusion | flops 403439616 | bytes 3670020 | tf_op jit(solution)/shard_map/sft,stn->fn/dot_general | solution.py:252
  81.3 4.5 %all-to-all-start.3 = ((bf16[4,2,96,512]{3,2,1,0:T(8,128)(2,1)}), bf16[4,2,96,512]{3,2,1,0:T(8,128)(2,1)S(1)}, u32[]{:S(2)}, u32[]{:S(2)}) async-start(bf16[4,2,96,512]{3,2,1,0:T(8,128)(2,1)} %bitcast.12), calls=%async_computation.3 | async-start | bytes 1572864 | tf_op jit(solution)/shard_map/all_to_all | solution.py:29
  85.8 8.0 %all-gather.3 = f32[192,128]{1,0:T(8,128)S(1)} all-gather(f32[96,128]{1,0:T(8,128)S(1)} %slice_add_fusion.1), channel_id=5, replica_groups={{0,256},{64,320},{128,384},{192,448},{1,257},{65,321},{129,385},{193,44..., dimensions={0}, use_global_device_ids=true | all-gather | bytes 147456 | tf_op jit(solution)/shard_map/all_gather | solution.py:24
  93.9 0.7 bitcast_subtract_fusion.1
  94.5 3.0 %all-to-all-done.3 = bf16[4,2,96,512]{3,2,1,0:T(8,128)(2,1)S(1)} async-done(((bf16[4,2,96,512]{3,2,1,0:T(8,128)(2,1)}), bf16[4,2,96,512]{3,2,1,0:T(8,128)(2,1)S(1)}, u32[]{:S(2)}, u32[]{:S(2)}) %all-to-all-start.3) | async-done | bytes 786464 | tf_op jit(solution)/shard_map/all_to_all | solution.py:29
  97.7 22.2 %all_gather.41 = bf16[2,96,512]{2,1,0:T(8,128)(2,1)S(1)} all-gather(bf16[1,96,512]{2,1,0:T(8,128)(2,1)S(1)} %dynamic-slice_convert_fusion), channel_id=1, replica_groups=mesh['r'=8,'z'=2,'y'=4,'x'=4,'c'=2] {'z'}, dimensions={0}, use_global_device_ids=true | all-gather | bytes 294912 | tf_op jit(solution)/shard_map/all_gather | solution.py:263
  119.9 0.9 multiply_subtract_fusion
  (23 shorter events, 1.2 us)
Async XLA Ops:
  3.9 5.1 %copy-start.1 = (f32[1,96,512]{2,1,0:T(8,128)S(1)}, f32[1,96,512]{2,1,0:T(8,128)}, u32[]{:S(2)}) copy-start(f32[1,96,512]{2,1,0:T(8,128)} %param.11) | copy-start | bytes 589828
  3.9 36.7 %all-to-all-start = ((bf16[8,768,128]{2,1,0:T(8,128)(2,1)}), bf16[8,768,128]{2,1,0:T(8,128)(2,1)S(1)}, u32[]{:S(2)}, u32[]{:S(2)}) async-start(bf16[8,768,128]{2,1,0:T(8,128)(2,1)} %bitcast.48), calls=%async_computation | async-start | bytes 3145728 | tf_op jit(solution)/shard_map/all_to_all | solution.py:29
  27.7 18.8 %copy-start.4 = (f32[2,96,128]{2,1,0:T(8,128)S(1)}, f32[2,96,128]{2,1,0:T(8,128)}, u32[]{:S(2)}) copy-start(f32[2,96,128]{2,1,0:T(8,128)} %param.15) | copy-start | bytes 294916
  27.7 18.8 %copy-start.6 = (f32[1,2,96,128]{3,2,1,0:T(8,128)S(1)}, f32[1,2,96,128]{3,2,1,0:T(8,128)}, u32[]{:S(2)}) copy-start(f32[1,2,96,128]{3,2,1,0:T(8,128)} %param.14) | copy-start | bytes 294916
  42.0 5.5 %collective-permute-start = (bf16[4,128,512]{2,1,0:T(8,128)(2,1)}, bf16[4,128,512]{2,1,0:T(8,128)(2,1)S(1)}, u32[]{:S(2)}, u32[]{:S(2)}) collective-permute-start(bf16[4,128,512]{2,1,0:T(8,128)(2,1)} %convolution_convert_fusion), channel_id=1, source_target_pairs={{0,1},{1,0},{2,3},{3,2},{4,5},{5,4},{6,7},{7,6},{8,9},{9,8},{10,11... | collective-permute-start | bytes 1572872 | tf_op jit(solution)/shard_map/ppermute | solution.py:19
  47.1 14.5 %copy-start = (bf16[128,512]{1,0:T(8,128)(2,1)S(1)}, bf16[128,512]{1,0:T(8,128)(2,1)}, u32[]{:S(2)}) copy-start(bf16[128,512]{1,0:T(8,128)(2,1)} %target_ref.1) | copy-start | bytes 393220
  48.4 13.2 %all-to-all-start.1 = ((bf16[4,128,512]{2,1,0:T(8,128)(2,1)}), bf16[4,128,512]{2,1,0:T(8,128)(2,1)S(1)}, u32[]{:S(2)}, u32[]{:S(2)}) async-start(bf16[4,128,512]{2,1,0:T(8,128)(2,1)} %shard_map.129), calls=%async_computation.1 | async-start | bytes 1048576 | tf_op jit(solution)/shard_map/all_to_all | solution.py:29
  62.5 11.1 %all-to-all-start.2 = ((bf16[4,128,512]{2,1,0:T(8,128)(2,1)}), bf16[4,128,512]{2,1,0:T(8,128)(2,1)S(1)}, u32[]{:S(2)}, u32[]{:S(2)}) async-start(bf16[4,128,512]{2,1,0:T(8,128)(2,1)} %shard_map.130), calls=%async_computation.2 | async-start | bytes 1048576 | tf_op jit(solution)/shard_map/all_to_all | solution.py:29
  73.7 6.2 %collective-permute-start.1 = (bf16[4,128,512]{2,1,0:T(8,128)(2,1)S(1)}, bf16[4,128,512]{2,1,0:T(8,128)(2,1)S(1)}, u32[]{:S(2)}, u32[]{:S(2)}) collective-permute-start(bf16[4,128,512]{2,1,0:T(8,128)(2,1)S(1)} %all-to-all-done.2), channel_id=1, source_target_pairs={{0,1},{1,0},{2,3},{3,2},{4,5},{5,4},{6,7},{7,6},{8,9},{9,8},{10,11... | collective-permute-start | bytes 1572872 | tf_op jit(solution)/shard_map/ppermute | solution.py:19
  81.3 12.5 %copy-start.5 = (f32[2,96,128]{2,1,0:T(8,128)S(1)}, f32[2,96,128]{2,1,0:T(8,128)}, u32[]{:S(2)}) copy-start(f32[2,96,128]{2,1,0:T(8,128)} %param.16) | copy-start | bytes 294916
  81.3 38.6 %copy-start.2 = (f32[1,96,512]{2,1,0:T(8,128)S(1)}, f32[1,96,512]{2,1,0:T(8,128)}, u32[]{:S(2)}) copy-start(f32[1,96,512]{2,1,0:T(8,128)} %param.13) | copy-start | bytes 589828
  81.3 38.6 %copy-start.3 = (f32[1,96,512]{2,1,0:T(8,128)S(1)}, f32[1,96,512]{2,1,0:T(8,128)}, u32[]{:S(2)}) copy-start(f32[1,96,512]{2,1,0:T(8,128)} %param.12) | copy-start | bytes 589828
  81.3 16.2 %all-to-all-start.3 = ((bf16[4,2,96,512]{3,2,1,0:T(8,128)(2,1)}), bf16[4,2,96,512]{3,2,1,0:T(8,128)(2,1)S(1)}, u32[]{:S(2)}, u32[]{:S(2)}) async-start(bf16[4,2,96,512]{3,2,1,0:T(8,128)(2,1)} %bitcast.12), calls=%async_computation.3 | async-start | bytes 1572864 | tf_op jit(solution)/shard_map/all_to_all | solution.py:29

commit v6 on v5

--- a/solution.py
+++ b/solution.py
@@ -240,7 +240,6 @@
     send = jnp.einsum("sft,fn->stn", theirs, low, preferred_element_type=f32).astype(bf16)
     part = jnp.einsum("sft,fn->stn", mine, low, preferred_element_type=f32)
     part = add_blocks(part, swap(send, "c"))
-    part, delta = lax.optimization_barrier((part, delta))
     part, delta = lax.optimization_barrier((exchange(part, "x"), pair_sum(delta, "r", 1)))
     factor = 1.0 / math.sqrt(tokens * nz * ny * nx * nc)
     cotangent = cotangents(factor, part, targets)

time: 121 us -> 121 us (level)
  no operation moved by 1% of the time
where the time goes in v6:
time: 121 us
  blocking collectives  70.1 us (58%)
  starting transfers between devices  25.8 us (21%)
  waiting for transfers between devices  12.5 us (10%)
  Pallas kernels  5.01 us (4%)
  matrix products  4.05 us (3%)
  other arithmetic  1.7 us (1%)
  between operations  1.42 us (1%)
    all_gather x1, blocking collectives, on_device(): came = lax.dynamic_index_in_dim(lax.all_gather(sent, 'z'), 1 - z, 0, False)  22.2 us
    all_gather x1, blocking collectives, on_device(): low = lax.all_gather(master.astype(bf16), 'z')  18.6 us
    all_to_all x4, starting transfers between devices, exchange(): return lax.all_to_all(blocks, axes, split_axis=0, concat_axis=0, tiled=True)  17.4 us
    all_gather x3, blocking collectives, pair_sum(): both = lax.all_gather(block, axis, axis_index_groups=groups)  16.5 us
    all_gather x1, blocking collectives, on_device(): low = lax.all_gather(low, 'y').reshape(group, columns)  12.8 us
    all_to_all x4, waiting for transfers between devices, exchange(): return lax.all_to_all(blocks, axes, split_axis=0, concat_axis=0, tiled=True)  10.4 us
    ppermute x2, starting transfers between devices, swap(): return lax.ppermute(block, axis, [(i, i ^ distance) for i in range(size)])  8.45 us
    pallas_call x1, Pallas kernels, normed_blocks(): pl.pallas_call(functools.partial(norm_kernel, sizes), out_shape=jax.Shape...  3.27 us
  transfers between devices with their start and end apart: 6, of which 5 were waited for; matrix products, arithmetic and copies ran while one was open for 2% of the time, Pallas kernels for 0%

profile of v6, /device:TPU:33, one launch (start us, length us, event | category | flops | bytes accessed | tf_op | source)
XLA Modules:
  0.0 120.6 jit_solution(5264657014925563181)
XLA Ops:
  0.6 3.3 %shard_map.128 = bf16[8,4,2,96,128]{4,3,2,1,0:T(8,128)(2,1)} custom-call(bf16[128,6144]{1,0:T(8,128)(2,1)} %act_ref.1), custom_call_target="tpu_custom_call" | custom-call | flops 6291456 | bytes 3145728 | tf_op jit(solution)/shard_map/pallas_call | solution.py:187
  3.9 5.1 %all-to-all-start = ((bf16[8,768,128]{2,1,0:T(8,128)(2,1)}), bf16[8,768,128]{2,1,0:T(8,128)(2,1)S(1)}, u32[]{:S(2)}, u32[]{:S(2)}) async-start(bf16[8,768,128]{2,1,0:T(8,128)(2,1)} %bitcast.49), calls=%async_computation | async-start | bytes 3145728 | tf_op jit(solution)/shard_map/all_to_all | solution.py:29
  9.1 18.6 %all_gather.30 = bf16[2,96,512]{2,1,0:T(8,128)(2,1)S(1)} all-gather(bf16[1,96,512]{2,1,0:T(8,128)(2,1)S(1)} %convert_element_type.26), channel_id=1, replica_groups=mesh['r'=8,'z'=2,'y'=4,'x'=4,'c'=2] {'z'}, dimensions={0}, use_global_device_ids=true | all-gather | bytes 294912 | tf_op jit(solution)/shard_map/all_gather | solution.py:230
  27.7 12.8 %all-gather = bf16[8,96,512]{2,1,0:T(8,128)(2,1)S(1)} all-gather(bf16[2,96,512]{2,1,0:T(8,128)(2,1)S(1)} %all_gather.30), channel_id=2, replica_groups=mesh['r'=8,'z'=2,'y'=4,'x'=4,'c'=2] {'y'}, dimensions={0}, use_global_device_ids=true | all-gather | bytes 983040 | tf_op jit(solution)/shard_map/all_gather | solution.py:231
  40.5 1.4 %convolution_convert_fusion = bf16[4,128,512]{2,1,0:T(8,128)(2,1)} fusion(bf16[768,512,1]{1,0,2:T(8,128)(2,1)S(1)} %bitcast.47, bf16[4,2,768,128]{3,2,1,0:T(8,128)(2,1)S(1)} %bitcast.43, s32[]{:T(128)S(6)} %select_n.23), kind=kOutput, calls=%fused_computation.3 | convolution fusion | flops 402915328 | bytes 2097156 | tf_op jit(solution)/shard_map/sft,fn->stn/dot_general | solution.py:240
  41.9 3.8 %collective-permute-start = (bf16[4,128,512]{2,1,0:T(8,128)(2,1)}, bf16[4,128,512]{2,1,0:T(8,128)(2,1)S(1)}, u32[]{:S(2)}, u32[]{:S(2)}) collective-permute-start(bf16[4,128,512]{2,1,0:T(8,128)(2,1)} %convolution_convert_fusion), channel_id=1, source_target_pairs={{0,1},{1,0},{2,3},{3,2},{4,5},{5,4},{6,7},{7,6},{8,9},{9,8},{10,11... | collective-permute-start | bytes 1572872 | tf_op jit(solution)/shard_map/ppermute | solution.py:19
  46.3 1.1 collective-permute-done.came_ref
  47.4 0.9 shard_map.129
  48.3 4.3 %all-to-all-start.1 = ((bf16[4,128,512]{2,1,0:T(8,128)(2,1)}), bf16[4,128,512]{2,1,0:T(8,128)(2,1)S(1)}, u32[]{:S(2)}, u32[]{:S(2)}) async-start(bf16[4,128,512]{2,1,0:T(8,128)(2,1)} %shard_map.129), calls=%async_computation.1 | async-start | bytes 1048576 | tf_op jit(solution)/shard_map/all_to_all | solution.py:29
  53.3 3.9 %all_gather.33 = f32[2,96,128]{2,1,0:T(8,128)S(1)} all-gather(f32[1,96,128]{2,1,0:T(8,128)S(1)} %bitcast_subtract_fusion.1), channel_id=1, replica_groups={{0,64},{128,192},{256,320},{384,448},{1,65},{129,193},{257,321},{385,44..., dimensions={0}, use_global_device_ids=true | all-gather | bytes 147456 | tf_op jit(solution)/shard_map/all_gather | solution.py:24
  57.2 4.3 %all-to-all-done.1.part_ref = bf16[4,128,512]{2,1,0:T(8,128)(2,1)S(1)} async-done(((bf16[4,128,512]{2,1,0:T(8,128)(2,1)}), bf16[4,128,512]{2,1,0:T(8,128)(2,1)S(1)}, u32[]{:S(2)}, u32[]{:S(2)}) %all-to-all-start.1) | async-done | bytes 524320 | tf_op jit(solution)/shard_map/all_to_all | solution.py:29
  61.5 0.9 shard_map.130
  62.4 3.5 %all-to-all-start.2 = ((bf16[4,128,512]{2,1,0:T(8,128)(2,1)}), bf16[4,128,512]{2,1,0:T(8,128)(2,1)S(1)}, u32[]{:S(2)}, u32[]{:S(2)}) async-start(bf16[4,128,512]{2,1,0:T(8,128)(2,1)} %shard_map.130), calls=%async_computation.2 | async-start | bytes 1048576 | tf_op jit(solution)/shard_map/all_to_all | solution.py:29
  65.9 4.5 %all-gather.1 = f32[192,128]{1,0:T(8,128)S(1)} all-gather(f32[96,128]{1,0:T(8,128)S(1)} %fusion.13), channel_id=3, replica_groups={{0,128},{64,192},{256,384},{320,448},{1,129},{65,193},{257,385},{321,44..., dimensions={0}, use_global_device_ids=true | all-gather | bytes 147456 | tf_op jit(solution)/shard_map/all_gather | solution.py:24
  70.4 3.1 %all-to-all-done.2 = bf16[4,128,512]{2,1,0:T(8,128)(2,1)S(1)} async-done(((bf16[4,128,512]{2,1,0:T(8,128)(2,1)}), bf16[4,128,512]{2,1,0:T(8,128)(2,1)S(1)}, u32[]{:S(2)}, u32[]{:S(2)}) %all-to-all-start.2) | async-done | bytes 524320 | tf_op jit(solution)/shard_map/all_to_all | solution.py:29
  73.5 4.6 %collective-permute-start.1 = (bf16[4,128,512]{2,1,0:T(8,128)(2,1)S(1)}, bf16[4,128,512]{2,1,0:T(8,128)(2,1)S(1)}, u32[]{:S(2)}, u32[]{:S(2)}) collective-permute-start(bf16[4,128,512]{2,1,0:T(8,128)(2,1)S(1)} %all-to-all-done.2), channel_id=1, source_target_pairs={{0,1},{1,0},{2,3},{3,2},{4,5},{5,4},{6,7},{7,6},{8,9},{9,8},{10,11... | collective-permute-start | bytes 1572872 | tf_op jit(solution)/shard_map/ppermute | solution.py:19
  78.7 0.9 collective-permute-done.1
  79.7 1.5 %fusion = bf16[768,512]{1,0:T(8,128)(2,1)} fusion(f32[768,512,1]{1,0,2:T(8,128)S(1)} %fusion.3, bf16[4,128,512]{2,1,0:T(8,128)(2,1)S(1)} %collective-permute-done.1, bf16[4,2,768,128]{3,2,1,0:T(8,128)(2,1)S(1)} %bitcast.46, s32[]{:T(128)S(6)} %select_n.23), kind=kOutput, calls=%fused_computation.1 | convolution fusion | flops 403439616 | bytes 3670020 | tf_op jit(solution)/shard_map/sft,stn->fn/dot_general | solution.py:251
  81.2 4.5 %all-to-all-start.3 = ((bf16[4,2,96,512]{3,2,1,0:T(8,128)(2,1)}), bf16[4,2,96,512]{3,2,1,0:T(8,128)(2,1)S(1)}, u32[]{:S(2)}, u32[]{:S(2)}) async-start(bf16[4,2,96,512]{3,2,1,0:T(8,128)(2,1)} %bitcast.12), calls=%async_computation.3 | async-start | bytes 1572864 | tf_op jit(solution)/shard_map/all_to_all | solution.py:29
  85.7 8.0 %all-gather.2 = f32[192,128]{1,0:T(8,128)S(1)} all-gather(f32[96,128]{1,0:T(8,128)S(1)} %slice_add_fusion.1), channel_id=4, replica_groups={{0,256},{64,320},{128,384},{192,448},{1,257},{65,321},{129,385},{193,44..., dimensions={0}, use_global_device_ids=true | all-gather | bytes 147456 | tf_op jit(solution)/shard_map/all_gather | solution.py:24
  93.7 0.7 bitcast_subtract_fusion
  94.4 3.0 %all-to-all-done.3 = bf16[4,2,96,512]{3,2,1,0:T(8,128)(2,1)S(1)} async-done(((bf16[4,2,96,512]{3,2,1,0:T(8,128)(2,1)}), bf16[4,2,96,512]{3,2,1,0:T(8,128)(2,1)S(1)}, u32[]{:S(2)}, u32[]{:S(2)}) %all-to-all-start.3) | async-done | bytes 786464 | tf_op jit(solution)/shard_map/all_to_all | solution.py:29
  97.5 22.2 %all_gather.38 = bf16[2,96,512]{2,1,0:T(8,128)(2,1)S(1)} all-gather(bf16[1,96,512]{2,1,0:T(8,128)(2,1)S(1)} %dynamic-slice_convert_fusion), channel_id=1, replica_groups=mesh['r'=8,'z'=2,'y'=4,'x'=4,'c'=2] {'z'}, dimensions={0}, use_global_device_ids=true | all-gather | bytes 294912 | tf_op jit(solution)/shard_map/all_gather | solution.py:262
  119.7 0.9 multiply_subtract_fusion
  (23 shorter events, 1.4 us)
Async XLA Ops:
  3.9 5.1 %copy-start.1 = (f32[1,96,512]{2,1,0:T(8,128)S(1)}, f32[1,96,512]{2,1,0:T(8,128)}, u32[]{:S(2)}) copy-start(f32[1,96,512]{2,1,0:T(8,128)} %param.11) | copy-start | bytes 589828
  3.9 36.6 %all-to-all-start = ((bf16[8,768,128]{2,1,0:T(8,128)(2,1)}), bf16[8,768,128]{2,1,0:T(8,128)(2,1)S(1)}, u32[]{:S(2)}, u32[]{:S(2)}) async-start(bf16[8,768,128]{2,1,0:T(8,128)(2,1)} %bitcast.49), calls=%async_computation | async-start | bytes 3145728 | tf_op jit(solution)/shard_map/all_to_all | solution.py:29
  41.9 5.5 %collective-permute-start = (bf16[4,128,512]{2,1,0:T(8,128)(2,1)}, bf16[4,128,512]{2,1,0:T(8,128)(2,1)S(1)}, u32[]{:S(2)}, u32[]{:S(2)}) collective-permute-start(bf16[4,128,512]{2,1,0:T(8,128)(2,1)} %convolution_convert_fusion), channel_id=1, source_target_pairs={{0,1},{1,0},{2,3},{3,2},{4,5},{5,4},{6,7},{7,6},{8,9},{9,8},{10,11... | collective-permute-start | bytes 1572872 | tf_op jit(solution)/shard_map/ppermute | solution.py:19
  46.3 6.9 %copy-start.4 = (f32[2,96,128]{2,1,0:T(8,128)S(1)}, f32[2,96,128]{2,1,0:T(8,128)}, u32[]{:S(2)}) copy-start(f32[2,96,128]{2,1,0:T(8,128)} %param.15) | copy-start | bytes 294916
  46.3 6.9 %copy-start.6 = (f32[1,2,96,128]{3,2,1,0:T(8,128)S(1)}, f32[1,2,96,128]{3,2,1,0:T(8,128)}, u32[]{:S(2)}) copy-start(f32[1,2,96,128]{3,2,1,0:T(8,128)} %param.14) | copy-start | bytes 294916
  46.3 15.2 %copy-start = (bf16[128,512]{1,0:T(8,128)(2,1)S(1)}, bf16[128,512]{1,0:T(8,128)(2,1)}, u32[]{:S(2)}) copy-start(bf16[128,512]{1,0:T(8,128)(2,1)} %target_ref.1) | copy-start | bytes 393220
  48.3 13.2 %all-to-all-start.1 = ((bf16[4,128,512]{2,1,0:T(8,128)(2,1)}), bf16[4,128,512]{2,1,0:T(8,128)(2,1)S(1)}, u32[]{:S(2)}, u32[]{:S(2)}) async-start(bf16[4,128,512]{2,1,0:T(8,128)(2,1)} %shard_map.129), calls=%async_computation.1 | async-start | bytes 1048576 | tf_op jit(solution)/shard_map/all_to_all | solution.py:29
  62.4 11.1 %all-to-all-start.2 = ((bf16[4,128,512]{2,1,0:T(8,128)(2,1)}), bf16[4,128,512]{2,1,0:T(8,128)(2,1)S(1)}, u32[]{:S(2)}, u32[]{:S(2)}) async-start(bf16[4,128,512]{2,1,0:T(8,128)(2,1)} %shard_map.130), calls=%async_computation.2 | async-start | bytes 1048576 | tf_op jit(solution)/shard_map/all_to_all | solution.py:29
  73.5 6.2 %collective-permute-start.1 = (bf16[4,128,512]{2,1,0:T(8,128)(2,1)S(1)}, bf16[4,128,512]{2,1,0:T(8,128)(2,1)S(1)}, u32[]{:S(2)}, u32[]{:S(2)}) collective-permute-start(bf16[4,128,512]{2,1,0:T(8,128)(2,1)S(1)} %all-to-all-done.2), channel_id=1, source_target_pairs={{0,1},{1,0},{2,3},{3,2},{4,5},{5,4},{6,7},{7,6},{8,9},{9,8},{10,11... | collective-permute-start | bytes 1572872 | tf_op jit(solution)/shard_map/ppermute | solution.py:19
  81.2 12.5 %copy-start.5 = (f32[2,96,128]{2,1,0:T(8,128)S(1)}, f32[2,96,128]{2,1,0:T(8,128)}, u32[]{:S(2)}) copy-start(f32[2,96,128]{2,1,0:T(8,128)} %param.16) | copy-start | bytes 294916
  81.2 38.6 %copy-start.2 = (f32[1,96,512]{2,1,0:T(8,128)S(1)}, f32[1,96,512]{2,1,0:T(8,128)}, u32[]{:S(2)}) copy-start(f32[1,96,512]{2,1,0:T(8,128)} %param.13) | copy-start | bytes 589828
  81.2 38.6 %copy-start.3 = (f32[1,96,512]{2,1,0:T(8,128)S(1)}, f32[1,96,512]{2,1,0:T(8,128)}, u32[]{:S(2)}) copy-start(f32[1,96,512]{2,1,0:T(8,128)} %param.12) | copy-start | bytes 589828
  81.2 16.2 %all-to-all-start.3 = ((bf16[4,2,96,512]{3,2,1,0:T(8,128)(2,1)}), bf16[4,2,96,512]{3,2,1,0:T(8,128)(2,1)S(1)}, u32[]{:S(2)}, u32[]{:S(2)}) async-start(bf16[4,2,96,512]{3,2,1,0:T(8,128)(2,1)} %bitcast.12), calls=%async_computation.3 | async-start | bytes 1572864 | tf_op jit(solution)/shard_map/all_to_all | solution.py:29

commit v7 on v6

--- a/solution.py
+++ b/solution.py
@@ -256,11 +256,11 @@
     new_momentum = 0.9 * moment_part + mean_delta
     new_global = global_part - 0.7 * (mean_delta + 0.9 * new_momentum)
     grad, new_global, new_momentum = lax.optimization_barrier((grad, new_global, new_momentum))
-    grad = jnp.sum(grad.astype(f32), axis=0)
-    sent = lax.dynamic_index_in_dim(grad, 1 - z, 0, False).astype(bf16)
-    kept = lax.dynamic_index_in_dim(grad, z, 0, False)
-    came = lax.dynamic_index_in_dim(lax.all_gather(sent, "z"), 1 - z, 0, False)
-    gradient = kept + came.astype(f32)
+    sent = jnp.sum(lax.dynamic_index_in_dim(grad, 1 - z, 1, False).astype(f32), axis=0)
+    came = lax.all_gather(sent.astype(bf16), "z")
+    came, grad = lax.optimization_barrier((came, grad))
+    kept = jnp.sum(lax.dynamic_index_in_dim(grad, z, 1, False).astype(f32), axis=0)
+    gradient = kept + lax.dynamic_index_in_dim(came, 1 - z, 0, False).astype(f32)
 
     new_first = 0.9 * first_moment[0] + 0.1 * gradient
     new_second = 0.95 * second_moment[0] + 0.05 * gradient * gradient

time: 121 us -> 121 us (level)
  no operation moved by 1% of the time
where the time goes in v7:
time: 121 us
  blocking collectives  70.1 us (58%)
  starting transfers between devices  25.8 us (21%)
  waiting for transfers between devices  12.5 us (10%)
  Pallas kernels  5.06 us (4%)
  matrix products  4.04 us (3%)
  other arithmetic  1.69 us (1%)
  between operations  1.43 us (1%)
    all_gather x1, blocking collectives, on_device(): came = lax.all_gather(sent.astype(bf16), 'z')  22.2 us
    all_gather x1, blocking collectives, on_device(): low = lax.all_gather(master.astype(bf16), 'z')  18.6 us
    all_to_all x4, starting transfers between devices, exchange(): return lax.all_to_all(blocks, axes, split_axis=0, concat_axis=0, tiled=True)  17.4 us
    all_gather x3, blocking collectives, pair_sum(): both = lax.all_gather(block, axis, axis_index_groups=groups)  16.5 us
    all_gather x1, blocking collectives, on_device(): low = lax.all_gather(low, 'y').reshape(group, columns)  12.8 us
    all_to_all x4, waiting for transfers between devices, exchange(): return lax.all_to_all(blocks, axes, split_axis=0, concat_axis=0, tiled=True)  10.4 us
    ppermute x2, starting transfers between devices, swap(): return lax.ppermute(block, axis, [(i, i ^ distance) for i in range(size)])  8.45 us
    pallas_call x1, Pallas kernels, normed_blocks(): pl.pallas_call(functools.partial(norm_kernel, sizes), out_shape=jax.Shape...  3.32 us
  transfers between devices with their start and end apart: 6, of which 5 were waited for; matrix products, arithmetic and copies ran while one was open for 2% of the time, Pallas kernels for 0%

profile of v7, /device:TPU:33, one launch (start us, length us, event | category | flops | bytes accessed | tf_op | source)
XLA Modules:
  0.0 120.7 jit_solution(886431480894018178)
XLA Ops:
  0.6 3.3 %shard_map.128 = bf16[8,4,2,96,128]{4,3,2,1,0:T(8,128)(2,1)} custom-call(bf16[128,6144]{1,0:T(8,128)(2,1)} %act_ref.1), custom_call_target="tpu_custom_call" | custom-call | flops 6291456 | bytes 3145728 | tf_op jit(solution)/shard_map/pallas_call | solution.py:187
  4.0 5.1 %all-to-all-start = ((bf16[8,768,128]{2,1,0:T(8,128)(2,1)}), bf16[8,768,128]{2,1,0:T(8,128)(2,1)S(1)}, u32[]{:S(2)}, u32[]{:S(2)}) async-start(bf16[8,768,128]{2,1,0:T(8,128)(2,1)} %bitcast.58), calls=%async_computation | async-start | bytes 3145728 | tf_op jit(solution)/shard_map/all_to_all | solution.py:29
  9.1 18.6 %all_gather.32 = bf16[2,96,512]{2,1,0:T(8,128)(2,1)S(1)} all-gather(bf16[1,96,512]{2,1,0:T(8,128)(2,1)S(1)} %convert_element_type.25), channel_id=1, replica_groups=mesh['r'=8,'z'=2,'y'=4,'x'=4,'c'=2] {'z'}, dimensions={0}, use_global_device_ids=true | all-gather | bytes 294912 | tf_op jit(solution)/shard_map/all_gather | solution.py:230
  27.7 12.8 %all-gather = bf16[8,96,512]{2,1,0:T(8,128)(2,1)S(1)} all-gather(bf16[2,96,512]{2,1,0:T(8,128)(2,1)S(1)} %all_gather.32), channel_id=2, replica_groups=mesh['r'=8,'z'=2,'y'=4,'x'=4,'c'=2] {'y'}, dimensions={0}, use_global_device_ids=true | all-gather | bytes 983040 | tf_op jit(solution)/shard_map/all_gather | solution.py:231
  40.5 1.4 %convolution_convert_fusion = bf16[4,128,512]{2,1,0:T(8,128)(2,1)} fusion(bf16[768,512,1]{1,0,2:T(8,128)(2,1)S(1)} %bitcast.56, bf16[4,2,768,128]{3,2,1,0:T(8,128)(2,1)S(1)} %bitcast.52, s32[]{:T(128)S(6)} %select_n.23), kind=kOutput, calls=%fused_computation.2 | convolution fusion | flops 402915328 | bytes 2097156 | tf_op jit(solution)/shard_map/sft,fn->stn/dot_general | solution.py:240
  41.9 3.8 %collective-permute-start = (bf16[4,128,512]{2,1,0:T(8,128)(2,1)}, bf16[4,128,512]{2,1,0:T(8,128)(2,1)S(1)}, u32[]{:S(2)}, u32[]{:S(2)}) collective-permute-start(bf16[4,128,512]{2,1,0:T(8,128)(2,1)} %convolution_convert_fusion), channel_id=1, source_target_pairs={{0,1},{1,0},{2,3},{3,2},{4,5},{5,4},{6,7},{7,6},{8,9},{9,8},{10,11... | collective-permute-start | bytes 1572872 | tf_op jit(solution)/shard_map/ppermute | solution.py:19
  46.4 1.1 collective-permute-done.came_ref
  47.5 0.9 shard_map.129
  48.3 4.3 %all-to-all-start.1 = ((bf16[4,128,512]{2,1,0:T(8,128)(2,1)}), bf16[4,128,512]{2,1,0:T(8,128)(2,1)S(1)}, u32[]{:S(2)}, u32[]{:S(2)}) async-start(bf16[4,128,512]{2,1,0:T(8,128)(2,1)} %shard_map.129), calls=%async_computation.1 | async-start | bytes 1048576 | tf_op jit(solution)/shard_map/all_to_all | solution.py:29
  53.3 3.9 %all_gather.35 = f32[2,96,128]{2,1,0:T(8,128)S(1)} all-gather(f32[1,96,128]{2,1,0:T(8,128)S(1)} %bitcast_subtract_fusion.1), channel_id=1, replica_groups={{0,64},{128,192},{256,320},{384,448},{1,65},{129,193},{257,321},{385,44..., dimensions={0}, use_global_device_ids=true | all-gather | bytes 147456 | tf_op jit(solution)/shard_map/all_gather | solution.py:24
  57.3 4.3 %all-to-all-done.1.part_ref = bf16[4,128,512]{2,1,0:T(8,128)(2,1)S(1)} async-done(((bf16[4,128,512]{2,1,0:T(8,128)(2,1)}), bf16[4,128,512]{2,1,0:T(8,128)(2,1)S(1)}, u32[]{:S(2)}, u32[]{:S(2)}) %all-to-all-start.1) | async-done | bytes 524320 | tf_op jit(solution)/shard_map/all_to_all | solution.py:29
  61.6 0.9 shard_map.130
  62.4 3.5 %all-to-all-start.2 = ((bf16[4,128,512]{2,1,0:T(8,128)(2,1)}), bf16[4,128,512]{2,1,0:T(8,128)(2,1)S(1)}, u32[]{:S(2)}, u32[]{:S(2)}) async-start(bf16[4,128,512]{2,1,0:T(8,128)(2,1)} %shard_map.130), calls=%async_computation.2 | async-start | bytes 1048576 | tf_op jit(solution)/shard_map/all_to_all | solution.py:29
  65.9 4.5 %all-gather.1 = f32[192,128]{1,0:T(8,128)S(1)} all-gather(f32[96,128]{1,0:T(8,128)S(1)} %fusion.13), channel_id=3, replica_groups={{0,128},{64,192},{256,384},{320,448},{1,129},{65,193},{257,385},{321,44..., dimensions={0}, use_global_device_ids=true | all-gather | bytes 147456 | tf_op jit(solution)/shard_map/all_gather | solution.py:24
  70.4 3.1 %all-to-all-done.2 = bf16[4,128,512]{2,1,0:T(8,128)(2,1)S(1)} async-done(((bf16[4,128,512]{2,1,0:T(8,128)(2,1)}), bf16[4,128,512]{2,1,0:T(8,128)(2,1)S(1)}, u32[]{:S(2)}, u32[]{:S(2)}) %all-to-all-start.2) | async-done | bytes 524320 | tf_op jit(solution)/shard_map/all_to_all | solution.py:29
  73.6 4.6 %collective-permute-start.1 = (bf16[4,128,512]{2,1,0:T(8,128)(2,1)S(1)}, bf16[4,128,512]{2,1,0:T(8,128)(2,1)S(1)}, u32[]{:S(2)}, u32[]{:S(2)}) collective-permute-start(bf16[4,128,512]{2,1,0:T(8,128)(2,1)S(1)} %all-to-all-done.2), channel_id=1, source_target_pairs={{0,1},{1,0},{2,3},{3,2},{4,5},{5,4},{6,7},{7,6},{8,9},{9,8},{10,11... | collective-permute-start | bytes 1572872 | tf_op jit(solution)/shard_map/ppermute | solution.py:19
  78.8 0.9 collective-permute-done.1
  79.7 1.5 %fusion = bf16[768,512]{1,0:T(8,128)(2,1)} fusion(f32[768,512,1]{1,0,2:T(8,128)S(1)} %fusion.3, bf16[4,128,512]{2,1,0:T(8,128)(2,1)S(1)} %collective-permute-done.1, bf16[4,2,768,128]{3,2,1,0:T(8,128)(2,1)S(1)} %bitcast.55, s32[]{:T(128)S(6)} %select_n.23), kind=kOutput, calls=%fused_computation.1 | convolution fusion | flops 403439616 | bytes 3670020 | tf_op jit(solution)/shard_map/sft,stn->fn/dot_general | solution.py:251
  81.2 4.5 %all-to-all-start.3 = ((bf16[4,2,96,512]{3,2,1,0:T(8,128)(2,1)}), bf16[4,2,96,512]{3,2,1,0:T(8,128)(2,1)S(1)}, u32[]{:S(2)}, u32[]{:S(2)}) async-start(bf16[4,2,96,512]{3,2,1,0:T(8,128)(2,1)} %bitcast.12), calls=%async_computation.3 | async-start | bytes 1572864 | tf_op jit(solution)/shard_map/all_to_all | solution.py:29
  85.7 8.0 %all-gather.2 = f32[192,128]{1,0:T(8,128)S(1)} all-gather(f32[96,128]{1,0:T(8,128)S(1)} %slice_add_fusion.1), channel_id=4, replica_groups={{0,256},{64,320},{128,384},{192,448},{1,257},{65,321},{129,385},{193,44..., dimensions={0}, use_global_device_ids=true | all-gather | bytes 147456 | tf_op jit(solution)/shard_map/all_gather | solution.py:24
  93.8 0.7 bitcast_subtract_fusion
  94.4 3.0 %all-to-all-done.3 = bf16[4,2,96,512]{3,2,1,0:T(8,128)(2,1)S(1)} async-done(((bf16[4,2,96,512]{3,2,1,0:T(8,128)(2,1)}), bf16[4,2,96,512]{3,2,1,0:T(8,128)(2,1)S(1)}, u32[]{:S(2)}, u32[]{:S(2)}) %all-to-all-start.3) | async-done | bytes 786464 | tf_op jit(solution)/shard_map/all_to_all | solution.py:29
  97.5 22.2 %all-gather.3 = bf16[192,512]{1,0:T(8,128)(2,1)S(1)} all-gather(bf16[96,512]{1,0:T(8,128)(2,1)S(1)} %dynamic-slice_reduce_fusion), channel_id=5, replica_groups=mesh['r'=8,'z'=2,'y'=4,'x'=4,'c'=2] {'z'}, dimensions={0}, use_global_device_ids=true | all-gather | bytes 294912 | tf_op jit(solution)/shard_map/all_gather | solution.py:260
  119.8 0.9 multiply_subtract_fusion
  (23 shorter events, 1.4 us)
Async XLA Ops:
  4.0 5.1 %copy-start.1 = (f32[1,96,512]{2,1,0:T(8,128)S(1)}, f32[1,96,512]{2,1,0:T(8,128)}, u32[]{:S(2)}) copy-start(f32[1,96,512]{2,1,0:T(8,128)} %param.11) | copy-start | bytes 589828
  4.0 36.6 %all-to-all-start = ((bf16[8,768,128]{2,1,0:T(8,128)(2,1)}), bf16[8,768,128]{2,1,0:T(8,128)(2,1)S(1)}, u32[]{:S(2)}, u32[]{:S(2)}) async-start(bf16[8,768,128]{2,1,0:T(8,128)(2,1)} %bitcast.58), calls=%async_computation | async-start | bytes 3145728 | tf_op jit(solution)/shard_map/all_to_all | solution.py:29
  41.9 5.5 %collective-permute-start = (bf16[4,128,512]{2,1,0:T(8,128)(2,1)}, bf16[4,128,512]{2,1,0:T(8,128)(2,1)S(1)}, u32[]{:S(2)}, u32[]{:S(2)}) collective-permute-start(bf16[4,128,512]{2,1,0:T(8,128)(2,1)} %convolution_convert_fusion), channel_id=1, source_target_pairs={{0,1},{1,0},{2,3},{3,2},{4,5},{5,4},{6,7},{7,6},{8,9},{9,8},{10,11... | collective-permute-start | bytes 1572872 | tf_op jit(solution)/shard_map/ppermute | solution.py:19
  46.4 7.0 %copy-start.4 = (f32[2,96,128]{2,1,0:T(8,128)S(1)}, f32[2,96,128]{2,1,0:T(8,128)}, u32[]{:S(2)}) copy-start(f32[2,96,128]{2,1,0:T(8,128)} %param.15) | copy-start | bytes 294916
  46.4 7.0 %copy-start.6 = (f32[1,2,96,128]{3,2,1,0:T(8,128)S(1)}, f32[1,2,96,128]{3,2,1,0:T(8,128)}, u32[]{:S(2)}) copy-start(f32[1,2,96,128]{3,2,1,0:T(8,128)} %param.14) | copy-start | bytes 294916
  46.4 15.2 %copy-start = (bf16[128,512]{1,0:T(8,128)(2,1)S(1)}, bf16[128,512]{1,0:T(8,128)(2,1)}, u32[]{:S(2)}) copy-start(bf16[128,512]{1,0:T(8,128)(2,1)} %target_ref.1) | copy-start | bytes 393220
  48.3 13.2 %all-to-all-start.1 = ((bf16[4,128,512]{2,1,0:T(8,128)(2,1)}), bf16[4,128,512]{2,1,0:T(8,128)(2,1)S(1)}, u32[]{:S(2)}, u32[]{:S(2)}) async-start(bf16[4,128,512]{2,1,0:T(8,128)(2,1)} %shard_map.129), calls=%async_computation.1 | async-start | bytes 1048576 | tf_op jit(solution)/shard_map/all_to_all | solution.py:29
  62.4 11.1 %all-to-all-start.2 = ((bf16[4,128,512]{2,1,0:T(8,128)(2,1)}), bf16[4,128,512]{2,1,0:T(8,128)(2,1)S(1)}, u32[]{:S(2)}, u32[]{:S(2)}) async-start(bf16[4,128,512]{2,1,0:T(8,128)(2,1)} %shard_map.130), calls=%async_computation.2 | async-start | bytes 1048576 | tf_op jit(solution)/shard_map/all_to_all | solution.py:29
  73.6 6.2 %collective-permute-start.1 = (bf16[4,128,512]{2,1,0:T(8,128)(2,1)S(1)}, bf16[4,128,512]{2,1,0:T(8,128)(2,1)S(1)}, u32[]{:S(2)}, u32[]{:S(2)}) collective-permute-start(bf16[4,128,512]{2,1,0:T(8,128)(2,1)S(1)} %all-to-all-done.2), channel_id=1, source_target_pairs={{0,1},{1,0},{2,3},{3,2},{4,5},{5,4},{6,7},{7,6},{8,9},{9,8},{10,11... | collective-permute-start | bytes 1572872 | tf_op jit(solution)/shard_map/ppermute | solution.py:19
  81.2 12.5 %copy-start.5 = (f32[2,96,128]{2,1,0:T(8,128)S(1)}, f32[2,96,128]{2,1,0:T(8,128)}, u32[]{:S(2)}) copy-start(f32[2,96,128]{2,1,0:T(8,128)} %param.16) | copy-start | bytes 294916
  81.2 38.5 %copy-start.2 = (f32[1,96,512]{2,1,0:T(8,128)S(1)}, f32[1,96,512]{2,1,0:T(8,128)}, u32[]{:S(2)}) copy-start(f32[1,96,512]{2,1,0:T(8,128)} %param.13) | copy-start | bytes 589828
  81.2 38.5 %copy-start.3 = (f32[1,96,512]{2,1,0:T(8,128)S(1)}, f32[1,96,512]{2,1,0:T(8,128)}, u32[]{:S(2)}) copy-start(f32[1,96,512]{2,1,0:T(8,128)} %param.12) | copy-start | bytes 589828
  81.2 16.2 %all-to-all-start.3 = ((bf16[4,2,96,512]{3,2,1,0:T(8,128)(2,1)}), bf16[4,2,96,512]{3,2,1,0:T(8,128)(2,1)S(1)}, u32[]{:S(2)}, u32[]{:S(2)}) async-start(bf16[4,2,96,512]{3,2,1,0:T(8,128)(2,1)} %bitcast.12), calls=%async_computation.3 | async-start | bytes 1572864 | tf_op jit(solution)/shard_map/all_to_all | solution.py:29

commit v8 on v6

--- a/solution.py
+++ b/solution.py
@@ -99,13 +99,8 @@
     )(activations)
 
 
-def add_kernel(kept_ref, came_ref, out_ref, block_ref, sems):
-    leave = [pltpu.make_async_copy(block_ref.at[i], out_ref.at[i], sems.at[i]) for i in range(out_ref.shape[0])]
-    for i, copy in enumerate(leave):
-        block_ref[i] = (kept_ref[i] + came_ref[i].astype(jnp.float32)).astype(block_ref.dtype)
-        copy.start()
-    for copy in leave:
-        copy.wait()
+def add_kernel(kept_ref, came_ref, out_ref):
+    out_ref[...] = (kept_ref[...] + came_ref[...].astype(jnp.float32)).astype(out_ref.dtype)
 
 
 def add_blocks(kept, came):
@@ -113,9 +108,8 @@
         add_kernel,
         out_shape=jax.ShapeDtypeStruct(came.shape, came.dtype),
         in_specs=[VMEM, VMEM],
-        out_specs=pl.BlockSpec(memory_space=pltpu.HBM),
-        scratch_shapes=[pltpu.VMEM(came.shape, came.dtype), pltpu.SemaphoreType.DMA((came.shape[0],))],
-        compiler_params=pltpu.CompilerParams(vmem_limit_bytes=16 * 2**20),
+        out_specs=VMEM,
+        compiler_params=pltpu.CompilerParams(vmem_limit_bytes=8 * 2**20),
         cost_estimate=pl.CostEstimate(flops=came.size, bytes_accessed=8 * came.size, transcendentals=0),
     )(kept, came)
 

time: 121 us -> 121 us (level)
  no operation moved by 1% of the time
where the time goes in v8:
time: 121 us
  blocking collectives  70.1 us (58%)
  starting transfers between devices  25.8 us (21%)
  waiting for transfers between devices  12.5 us (10%)
  Pallas kernels  5.04 us (4%)
  matrix products  4.05 us (3%)
  other arithmetic  1.7 us (1%)
  between operations  1.41 us (1%)
    all_gather x1, blocking collectives, on_device(): came = lax.dynamic_index_in_dim(lax.all_gather(sent, 'z'), 1 - z, 0, False)  22.2 us
    all_gather x1, blocking collectives, on_device(): low = lax.all_gather(master.astype(bf16), 'z')  18.6 us
    all_to_all x4, starting transfers between devices, exchange(): return lax.all_to_all(blocks, axes, split_axis=0, concat_axis=0, tiled=True)  17.4 us
    all_gather x3, blocking collectives, pair_sum(): both = lax.all_gather(block, axis, axis_index_groups=groups)  16.5 us
    all_gather x1, blocking collectives, on_device(): low = lax.all_gather(low, 'y').reshape(group, columns)  12.8 us
    all_to_all x4, waiting for transfers between devices, exchange(): return lax.all_to_all(blocks, axes, split_axis=0, concat_axis=0, tiled=True)  10.4 us
    ppermute x2, starting transfers between devices, swap(): return lax.ppermute(block, axis, [(i, i ^ distance) for i in range(size)])  8.45 us
    pallas_call x1, Pallas kernels, normed_blocks(): pl.pallas_call(functools.partial(norm_kernel, sizes), out_shape=jax.Shape...  3.27 us
  transfers between devices with their start and end apart: 6, of which 5 were waited for; matrix products, arithmetic and copies ran while one was open for 2% of the time, Pallas kernels for 0%

profile of v8, /device:TPU:33, one launch (start us, length us, event | category | flops | bytes accessed | tf_op | source)
XLA Modules:
  0.0 120.6 jit_solution(11864786190338149737)
XLA Ops:
  0.6 3.3 %shard_map.128 = bf16[8,4,2,96,128]{4,3,2,1,0:T(8,128)(2,1)} custom-call(bf16[128,6144]{1,0:T(8,128)(2,1)} %act_ref.1), custom_call_target="tpu_custom_call" | custom-call | flops 6291456 | bytes 3145728 | tf_op jit(solution)/shard_map/pallas_call | solution.py:181
  3.9 5.1 %all-to-all-start = ((bf16[8,768,128]{2,1,0:T(8,128)(2,1)}), bf16[8,768,128]{2,1,0:T(8,128)(2,1)S(1)}, u32[]{:S(2)}, u32[]{:S(2)}) async-start(bf16[8,768,128]{2,1,0:T(8,128)(2,1)} %bitcast.49), calls=%async_computation | async-start | bytes 3145728 | tf_op jit(solution)/shard_map/all_to_all | solution.py:29
  9.1 18.6 %all_gather.30 = bf16[2,96,512]{2,1,0:T(8,128)(2,1)S(1)} all-gather(bf16[1,96,512]{2,1,0:T(8,128)(2,1)S(1)} %convert_element_type.26), channel_id=1, replica_groups=mesh['r'=8,'z'=2,'y'=4,'x'=4,'c'=2] {'z'}, dimensions={0}, use_global_device_ids=true | all-gather | bytes 294912 | tf_op jit(solution)/shard_map/all_gather | solution.py:224
  27.7 12.8 %all-gather = bf16[8,96,512]{2,1,0:T(8,128)(2,1)S(1)} all-gather(bf16[2,96,512]{2,1,0:T(8,128)(2,1)S(1)} %all_gather.30), channel_id=2, replica_groups=mesh['r'=8,'z'=2,'y'=4,'x'=4,'c'=2] {'y'}, dimensions={0}, use_global_device_ids=true | all-gather | bytes 983040 | tf_op jit(solution)/shard_map/all_gather | solution.py:225
  40.5 1.4 %convolution_convert_fusion = bf16[4,128,512]{2,1,0:T(8,128)(2,1)} fusion(bf16[768,512,1]{1,0,2:T(8,128)(2,1)S(1)} %bitcast.47, bf16[4,2,768,128]{3,2,1,0:T(8,128)(2,1)S(1)} %bitcast.43, s32[]{:T(128)S(6)} %select_n.23), kind=kOutput, calls=%fused_computation.3 | convolution fusion | flops 402915328 | bytes 2097156 | tf_op jit(solution)/shard_map/sft,fn->stn/dot_general | solution.py:234
  41.9 3.8 %collective-permute-start = (bf16[4,128,512]{2,1,0:T(8,128)(2,1)}, bf16[4,128,512]{2,1,0:T(8,128)(2,1)S(1)}, u32[]{:S(2)}, u32[]{:S(2)}) collective-permute-start(bf16[4,128,512]{2,1,0:T(8,128)(2,1)} %convolution_convert_fusion), channel_id=1, source_target_pairs={{0,1},{1,0},{2,3},{3,2},{4,5},{5,4},{6,7},{7,6},{8,9},{9,8},{10,11... | collective-permute-start | bytes 1572872 | tf_op jit(solution)/shard_map/ppermute | solution.py:19
  46.3 1.1 collective-permute-done.came_ref
  47.4 0.9 shard_map.129
  48.3 4.3 %all-to-all-start.1 = ((bf16[4,128,512]{2,1,0:T(8,128)(2,1)}), bf16[4,128,512]{2,1,0:T(8,128)(2,1)S(1)}, u32[]{:S(2)}, u32[]{:S(2)}) async-start(bf16[4,128,512]{2,1,0:T(8,128)(2,1)} %shard_map.129), calls=%async_computation.1 | async-start | bytes 1048576 | tf_op jit(solution)/shard_map/all_to_all | solution.py:29
  53.3 3.9 %all_gather.33 = f32[2,96,128]{2,1,0:T(8,128)S(1)} all-gather(f32[1,96,128]{2,1,0:T(8,128)S(1)} %bitcast_subtract_fusion.1), channel_id=1, replica_groups={{0,64},{128,192},{256,320},{384,448},{1,65},{129,193},{257,321},{385,44..., dimensions={0}, use_global_device_ids=true | all-gather | bytes 147456 | tf_op jit(solution)/shard_map/all_gather | solution.py:24
  57.2 4.3 %all-to-all-done.1.part_ref = bf16[4,128,512]{2,1,0:T(8,128)(2,1)S(1)} async-done(((bf16[4,128,512]{2,1,0:T(8,128)(2,1)}), bf16[4,128,512]{2,1,0:T(8,128)(2,1)S(1)}, u32[]{:S(2)}, u32[]{:S(2)}) %all-to-all-start.1) | async-done | bytes 524320 | tf_op jit(solution)/shard_map/all_to_all | solution.py:29
  61.5 0.9 shard_map.130
  62.4 3.5 %all-to-all-start.2 = ((bf16[4,128,512]{2,1,0:T(8,128)(2,1)}), bf16[4,128,512]{2,1,0:T(8,128)(2,1)S(1)}, u32[]{:S(2)}, u32[]{:S(2)}) async-start(bf16[4,128,512]{2,1,0:T(8,128)(2,1)} %shard_map.130), calls=%async_computation.2 | async-start | bytes 1048576 | tf_op jit(solution)/shard_map/all_to_all | solution.py:29
  65.9 4.5 %all-gather.1 = f32[192,128]{1,0:T(8,128)S(1)} all-gather(f32[96,128]{1,0:T(8,128)S(1)} %fusion.13), channel_id=3, replica_groups={{0,128},{64,192},{256,384},{320,448},{1,129},{65,193},{257,385},{321,44..., dimensions={0}, use_global_device_ids=true | all-gather | bytes 147456 | tf_op jit(solution)/shard_map/all_gather | solution.py:24
  70.4 3.1 %all-to-all-done.2 = bf16[4,128,512]{2,1,0:T(8,128)(2,1)S(1)} async-done(((bf16[4,128,512]{2,1,0:T(8,128)(2,1)}), bf16[4,128,512]{2,1,0:T(8,128)(2,1)S(1)}, u32[]{:S(2)}, u32[]{:S(2)}) %all-to-all-start.2) | async-done | bytes 524320 | tf_op jit(solution)/shard_map/all_to_all | solution.py:29
  73.5 4.6 %collective-permute-start.1 = (bf16[4,128,512]{2,1,0:T(8,128)(2,1)S(1)}, bf16[4,128,512]{2,1,0:T(8,128)(2,1)S(1)}, u32[]{:S(2)}, u32[]{:S(2)}) collective-permute-start(bf16[4,128,512]{2,1,0:T(8,128)(2,1)S(1)} %all-to-all-done.2), channel_id=1, source_target_pairs={{0,1},{1,0},{2,3},{3,2},{4,5},{5,4},{6,7},{7,6},{8,9},{9,8},{10,11... | collective-permute-start | bytes 1572872 | tf_op jit(solution)/shard_map/ppermute | solution.py:19
  78.8 0.9 collective-permute-done.1
  79.7 1.5 %fusion = bf16[768,512]{1,0:T(8,128)(2,1)} fusion(f32[768,512,1]{1,0,2:T(8,128)S(1)} %fusion.3, bf16[4,128,512]{2,1,0:T(8,128)(2,1)S(1)} %collective-permute-done.1, bf16[4,2,768,128]{3,2,1,0:T(8,128)(2,1)S(1)} %bitcast.46, s32[]{:T(128)S(6)} %select_n.23), kind=kOutput, calls=%fused_computation.1 | convolution fusion | flops 403439616 | bytes 3670020 | tf_op jit(solution)/shard_map/sft,stn->fn/dot_general | solution.py:245
  81.2 4.5 %all-to-all-start.3 = ((bf16[4,2,96,512]{3,2,1,0:T(8,128)(2,1)}), bf16[4,2,96,512]{3,2,1,0:T(8,128)(2,1)S(1)}, u32[]{:S(2)}, u32[]{:S(2)}) async-start(bf16[4,2,96,512]{3,2,1,0:T(8,128)(2,1)} %bitcast.12), calls=%async_computation.3 | async-start | bytes 1572864 | tf_op jit(solution)/shard_map/all_to_all | solution.py:29
  85.7 8.0 %all-gather.2 = f32[192,128]{1,0:T(8,128)S(1)} all-gather(f32[96,128]{1,0:T(8,128)S(1)} %slice_add_fusion.1), channel_id=4, replica_groups={{0,256},{64,320},{128,384},{192,448},{1,257},{65,321},{129,385},{193,44..., dimensions={0}, use_global_device_ids=true | all-gather | bytes 147456 | tf_op jit(solution)/shard_map/all_gather | solution.py:24
  93.7 0.7 bitcast_subtract_fusion
  94.4 3.0 %all-to-all-done.3 = bf16[4,2,96,512]{3,2,1,0:T(8,128)(2,1)S(1)} async-done(((bf16[4,2,96,512]{3,2,1,0:T(8,128)(2,1)}), bf16[4,2,96,512]{3,2,1,0:T(8,128)(2,1)S(1)}, u32[]{:S(2)}, u32[]{:S(2)}) %all-to-all-start.3) | async-done | bytes 786464 | tf_op jit(solution)/shard_map/all_to_all | solution.py:29
  97.5 22.2 %all_gather.38 = bf16[2,96,512]{2,1,0:T(8,128)(2,1)S(1)} all-gather(bf16[1,96,512]{2,1,0:T(8,128)(2,1)S(1)} %dynamic-slice_convert_fusion), channel_id=1, replica_groups=mesh['r'=8,'z'=2,'y'=4,'x'=4,'c'=2] {'z'}, dimensions={0}, use_global_device_ids=true | all-gather | bytes 294912 | tf_op jit(solution)/shard_map/all_gather | solution.py:256
  119.8 0.9 multiply_subtract_fusion
  (23 shorter events, 1.4 us)
Async XLA Ops:
  3.9 5.1 %copy-start.1 = (f32[1,96,512]{2,1,0:T(8,128)S(1)}, f32[1,96,512]{2,1,0:T(8,128)}, u32[]{:S(2)}) copy-start(f32[1,96,512]{2,1,0:T(8,128)} %param.11) | copy-start | bytes 589828
  3.9 36.6 %all-to-all-start = ((bf16[8,768,128]{2,1,0:T(8,128)(2,1)}), bf16[8,768,128]{2,1,0:T(8,128)(2,1)S(1)}, u32[]{:S(2)}, u32[]{:S(2)}) async-start(bf16[8,768,128]{2,1,0:T(8,128)(2,1)} %bitcast.49), calls=%async_computation | async-start | bytes 3145728 | tf_op jit(solution)/shard_map/all_to_all | solution.py:29
  41.9 5.5 %collective-permute-start = (bf16[4,128,512]{2,1,0:T(8,128)(2,1)}, bf16[4,128,512]{2,1,0:T(8,128)(2,1)S(1)}, u32[]{:S(2)}, u32[]{:S(2)}) collective-permute-start(bf16[4,128,512]{2,1,0:T(8,128)(2,1)} %convolution_convert_fusion), channel_id=1, source_target_pairs={{0,1},{1,0},{2,3},{3,2},{4,5},{5,4},{6,7},{7,6},{8,9},{9,8},{10,11... | collective-permute-start | bytes 1572872 | tf_op jit(solution)/shard_map/ppermute | solution.py:19
  46.3 7.0 %copy-start.4 = (f32[2,96,128]{2,1,0:T(8,128)S(1)}, f32[2,96,128]{2,1,0:T(8,128)}, u32[]{:S(2)}) copy-start(f32[2,96,128]{2,1,0:T(8,128)} %param.15) | copy-start | bytes 294916
  46.3 7.0 %copy-start.6 = (f32[1,2,96,128]{3,2,1,0:T(8,128)S(1)}, f32[1,2,96,128]{3,2,1,0:T(8,128)}, u32[]{:S(2)}) copy-start(f32[1,2,96,128]{3,2,1,0:T(8,128)} %param.14) | copy-start | bytes 294916
  46.3 15.2 %copy-start = (bf16[128,512]{1,0:T(8,128)(2,1)S(1)}, bf16[128,512]{1,0:T(8,128)(2,1)}, u32[]{:S(2)}) copy-start(bf16[128,512]{1,0:T(8,128)(2,1)} %target_ref.1) | copy-start | bytes 393220
  48.3 13.2 %all-to-all-start.1 = ((bf16[4,128,512]{2,1,0:T(8,128)(2,1)}), bf16[4,128,512]{2,1,0:T(8,128)(2,1)S(1)}, u32[]{:S(2)}, u32[]{:S(2)}) async-start(bf16[4,128,512]{2,1,0:T(8,128)(2,1)} %shard_map.129), calls=%async_computation.1 | async-start | bytes 1048576 | tf_op jit(solution)/shard_map/all_to_all | solution.py:29
  62.4 11.1 %all-to-all-start.2 = ((bf16[4,128,512]{2,1,0:T(8,128)(2,1)}), bf16[4,128,512]{2,1,0:T(8,128)(2,1)S(1)}, u32[]{:S(2)}, u32[]{:S(2)}) async-start(bf16[4,128,512]{2,1,0:T(8,128)(2,1)} %shard_map.130), calls=%async_computation.2 | async-start | bytes 1048576 | tf_op jit(solution)/shard_map/all_to_all | solution.py:29
  73.5 6.2 %collective-permute-start.1 = (bf16[4,128,512]{2,1,0:T(8,128)(2,1)S(1)}, bf16[4,128,512]{2,1,0:T(8,128)(2,1)S(1)}, u32[]{:S(2)}, u32[]{:S(2)}) collective-permute-start(bf16[4,128,512]{2,1,0:T(8,128)(2,1)S(1)} %all-to-all-done.2), channel_id=1, source_target_pairs={{0,1},{1,0},{2,3},{3,2},{4,5},{5,4},{6,7},{7,6},{8,9},{9,8},{10,11... | collective-permute-start | bytes 1572872 | tf_op jit(solution)/shard_map/ppermute | solution.py:19
  81.2 12.5 %copy-start.5 = (f32[2,96,128]{2,1,0:T(8,128)S(1)}, f32[2,96,128]{2,1,0:T(8,128)}, u32[]{:S(2)}) copy-start(f32[2,96,128]{2,1,0:T(8,128)} %param.16) | copy-start | bytes 294916
  81.2 38.6 %copy-start.2 = (f32[1,96,512]{2,1,0:T(8,128)S(1)}, f32[1,96,512]{2,1,0:T(8,128)}, u32[]{:S(2)}) copy-start(f32[1,96,512]{2,1,0:T(8,128)} %param.13) | copy-start | bytes 589828
  81.2 38.6 %copy-start.3 = (f32[1,96,512]{2,1,0:T(8,128)S(1)}, f32[1,96,512]{2,1,0:T(8,128)}, u32[]{:S(2)}) copy-start(f32[1,96,512]{2,1,0:T(8,128)} %param.12) | copy-start | bytes 589828
  81.2 16.2 %all-to-all-start.3 = ((bf16[4,2,96,512]{3,2,1,0:T(8,128)(2,1)}), bf16[4,2,96,512]{3,2,1,0:T(8,128)(2,1)S(1)}, u32[]{:S(2)}, u32[]{:S(2)}) async-start(bf16[4,2,96,512]{3,2,1,0:T(8,128)(2,1)} %bitcast.12), calls=%async_computation.3 | async-start | bytes 1572864 | tf_op jit(solution)/shard_map/all_to_all | solution.py:29
